TPU v7x, 256 devices: a whole 4x4x8 slice. The times are simulated.
256 devices in a mesh: dp: 4 (over x), fsdp: 2 (over core), tp: 32 (over z, y).
Axes of the slice: x: 4, y: 4, z: 8, core: 2. Of those that a mesh axis runs over, the one named last changes fastest.
Arguments:
- momentum: float32 [4, 8192, 8192], P('dp', 'fsdp', 'tp'), may hold values from -90 to 90
- gradient: bfloat16 [4, 8192, 8192], P('dp', 'fsdp', 'tp'), may hold values from -6 to 6
- basis: float32 [8192, 512], P('tp', 'fsdp'), may hold values from -6 to 6
Outputs:
- new_momentum: float32 [4, 8192, 8192], P('dp', 'fsdp', 'tp')
- new_basis: float32 [8192, 512], P('tp', 'fsdp')
- update: bfloat16 [8192, 8192], P('fsdp', 'tp')
All inputs are finite; a program needn't handle non-finite values.
Results may differ from a plain program's by a relative error of at most 0.025.
Values may be sent and summed in bfloat16 or wider, within the bound.
A program may use at most 128 MiB of HBM per device.

v0:
```python
import jax
import jax.numpy as jnp
from jax import lax
from jax.sharding import PartitionSpec as P

D = 8192
R = 512


def orthonormal(left_part, gram):
    lower = jnp.linalg.cholesky(gram)
    inverse = jax.scipy.linalg.solve_triangular(
        lower, jnp.eye(gram.shape[0], dtype=jnp.float32), lower=True
    )
    ortho = jnp.dot(left_part, inverse.T, precision=lax.Precision.HIGHEST)
    return ortho.astype(jnp.bfloat16)


def shards(momentum, gradient, basis):
    buffer = momentum[0] + gradient[0].astype(jnp.float32)
    buffer_low = buffer.astype(jnp.bfloat16)
    basis_low = basis.astype(jnp.bfloat16)
    replicas = lax.axis_size("dp")
    rank_share = basis.shape[1]
    basis_full = lax.all_gather(basis_low, "fsdp", axis=1, tiled=True)
    share_left = lax.psum_scatter(
        jnp.dot(buffer_low, basis_full, preferred_element_type=jnp.float32),
        "tp",
        scatter_dimension=0,
        tiled=True,
    )
    left_mean = lax.psum(share_left.astype(jnp.bfloat16), "dp").astype(jnp.float32) / replicas
    gram = lax.psum(
        jnp.dot(left_mean.T, left_mean, precision=lax.Precision.HIGHEST), ("fsdp", "tp")
    )
    ortho_share = orthonormal(left_mean, gram)
    ortho_low = lax.all_gather(ortho_share, "tp", axis=0, tiled=True)
    width = basis.shape[0] * lax.axis_size("tp")
    partial_right = lax.dot_general(
        ortho_low, buffer_low, (((0,), (0,)), ((), ())), preferred_element_type=jnp.float32
    )
    summed_right = lax.psum(partial_right, "fsdp")
    right_mean = lax.psum(summed_right.astype(jnp.bfloat16), "dp").astype(jnp.float32) / replicas
    squares = lax.psum(jnp.sum(right_mean * right_mean, axis=1), "tp")
    next_rows = right_mean * (1.0 / jnp.sqrt(squares / width + 1e-05))[:, None]
    right_low = right_mean.astype(jnp.bfloat16)
    next_low = next_rows.astype(jnp.bfloat16)
    owned = lax.dynamic_slice_in_dim(next_rows, lax.axis_index("fsdp") * rank_share, rank_share, 0)
    new_basis = owned.T
    lowrank = jnp.dot(ortho_low, right_low, preferred_element_type=jnp.float32)
    new_momentum = (buffer - 0.05 * lowrank)[None]
    factor = D / jnp.sqrt(jnp.float32(R))
    update = (jnp.dot(ortho_low, next_low, preferred_element_type=jnp.float32) * factor).astype(
        jnp.bfloat16
    )
    return (new_momentum, new_basis, update)


def solution(mesh):
    in_specs = (P("dp", "fsdp", "tp"), P("dp", "fsdp", "tp"), P("tp", "fsdp"))
    out_specs = (P("dp", "fsdp", "tp"), P("tp", "fsdp"), P("fsdp", "tp"))
    return jax.shard_map(shards, mesh=mesh, in_specs=in_specs, out_specs=out_specs, check_vma=False)
```

profile of v0, /device:TPU:6, one launch (start us, length us, event | category | flops | bytes accessed | tf_op | source)
XLA Modules:
  0.0 862.9 jit_solution(16236747374213625117)
XLA Ops:
  7.2 1.0 convert_element_type.43
  8.2 2.0 all_gather.6
  10.2 7.3 fusion.55
  17.6 231.7 %reduce-scatter.2.cloned.1.call-done = f32[128,512]{1,0:T(8,128)} async-done(((f32[4096,512]{1,0:T(8,128)}), f32[128,512]{1,0:T(8,128)}) %reduce-scatter.2.cloned.1.call-update) | async-done | bytes 262160 | tf_op jit(solution)/shard_map/reduce_scatter | solution.py:26
  249.3 1.6 convert_element_type.44
  251.0 0.0 all-reduce.8.cloned.1.call-start
  251.0 44.9 %all-reduce.6.cloned.1.call-done = bf16[128,512]{1,0:T(8,128)(2,1)} async-done(((bf16[128,512]{1,0:T(8,128)(2,1)}), bf16[128,512]{1,0:T(8,128)(2,1)}) %all-reduce.6.cloned.1.call-update) | async-done | bytes 131088 | tf_op jit(solution)/shard_map/psum | solution.py:32
  295.9 3.0 fusion.27
  298.9 0.5 all-gather.2.cloned.1.call-start
  299.5 0.8 iota_compare_fusion
  300.2 0.1 fusion.22
  300.4 186.4 %all-reduce.8.cloned.1.call-done = f32[512,512]{0,1:T(8,128)} async-done(((f32[512,512]{0,1:T(8,128)}), f32[512,512]{0,1:T(8,128)}) %all-reduce.8.cloned.1.call-update) | async-done | bytes 1048592 | tf_op jit(solution)/shard_map/psum | solution.py:33
  486.8 1.6 copy.7
  488.3 1.4 fusion.10
  489.8 11.7 %cholesky.104 = f32[128,128]{1,0:T(8,128)S(1)} custom-call(f32[128,128]{1,0:T(8,128)S(1)} %cholesky.266), custom_call_target="Cholesky" | custom-call | tf_op jit(solution)/shard_map/jit(cholesky)/cholesky | solution.py:11
  501.6 9.8 %custom-call.31 = f32[1,128,128]{1,2,0:T(8,128)S(1)} custom-call(f32[1,128,128]{2,1,0:T(8,128)S(1)} %get-tuple-element.33), custom_call_target="InvertDiagBlocksLowerTriangular" | custom-call | tf_op jit(solution)/shard_map/jit(cholesky)/cholesky | solution.py:11
  511.4 0.1 cholesky.224
  511.5 0.3 constant_dynamic-update-slice_fusion.3
  511.8 0.3 convolution_subtract_fusion.3
  512.2 11.7 %cholesky.217 = f32[128,128]{1,0:T(8,128)S(1)} custom-call(f32[128,128]{1,0:T(8,128)S(1)} %cholesky.270), custom_call_target="Cholesky" | custom-call | tf_op jit(solution)/shard_map/jit(cholesky)/cholesky | solution.py:11
  523.9 10.0 %custom-call.32 = f32[1,128,128]{1,2,0:T(8,128)S(1)} custom-call(f32[1,128,128]{2,1,0:T(8,128)S(1)} %get-tuple-element.30), custom_call_target="InvertDiagBlocksLowerTriangular" | custom-call | tf_op jit(solution)/shard_map/jit(cholesky)/cholesky | solution.py:11
  533.9 0.3 convolution_dynamic-update-slice_fusion
  534.1 0.4 convolution_subtract_fusion.4
  534.5 11.7 %cholesky.238 = f32[128,128]{1,0:T(8,128)S(1)} custom-call(f32[128,128]{1,0:T(8,128)S(1)} %cholesky.275), custom_call_target="Cholesky" | custom-call | tf_op jit(solution)/shard_map/jit(cholesky)/cholesky | solution.py:11
  546.3 0.7 compare_reduce_fusion.1
  547.0 9.8 %custom-call.33 = f32[1,128,128]{1,2,0:T(8,128)S(1)} custom-call(f32[1,128,128]{2,1,0:T(8,128)S(1)} %get-tuple-element.27), custom_call_target="InvertDiagBlocksLowerTriangular" | custom-call | tf_op jit(solution)/shard_map/jit(cholesky)/cholesky | solution.py:11
  556.8 0.2 convolution_dynamic-update-slice_fusion.1
  557.0 0.4 convolution_subtract_fusion.5
  557.4 11.7 %cholesky.255 = f32[128,128]{1,0:T(8,128)S(1)} custom-call(f32[128,128]{1,0:T(8,128)S(1)} %convolution_subtract_fusion.5), custom_call_target="Cholesky" | custom-call | tf_op jit(solution)/shard_map/jit(cholesky)/cholesky | solution.py:11
  569.2 0.6 compare_reduce_fusion
  569.8 0.9 compare_reduce_fusion.2
  573.2 1.1 select_select_fusion
  574.3 14.2 %while.1 = (s32[]{:T(128)}, f32[512,512]{1,0:T(8,128)}, s32[4,2]{0,1:T(2,128)S(1)}, f32[4,128,128]{2,1,0:T(8,128)}, s32[]{:T(128)}) while((s32[]{:T(128)}, f32[512,512]{1,0:T(8,128)}, s32[4,2]{0,1:T(2,128)S(1)}, f32[4,128,128]{2,1,0:T(8,128)}, s32[]{:T(128)}) %tuple.32), condition=%wide.while_cond, body=%wide.while_body.sunk | while | flops 2 | bytes 132205 | solution.py:12
  574.3 0.1 constant_dynamic-slice_fusion.2
  574.4 0.6 fusion.67
  575.0 2.9 bitcast_dynamic-update-slice_fusion.2
  577.9 0.1 constant_dynamic-slice_fusion.2
  577.9 0.6 fusion.67
  578.5 2.9 bitcast_dynamic-update-slice_fusion.2
  581.4 0.1 constant_dynamic-slice_fusion.2
  581.5 0.6 fusion.67
  582.1 2.9 bitcast_dynamic-update-slice_fusion.2
  585.0 0.1 constant_dynamic-slice_fusion.2
  585.0 0.6 fusion.67
  585.6 2.8 bitcast_dynamic-update-slice_fusion.2
  588.5 40.1 %custom-call.34 = f32[4,128,128]{1,2,0:T(8,128)S(1)} custom-call(f32[4,128,128]{2,1,0:T(8,128)} %get-tuple-element.10), custom_call_target="InvertDiagBlocksLowerTriangular" | custom-call | tf_op jit(solution)/shard_map/jit(_solve_triangular)/triangular_solve | solution.py:12
  628.6 1.1 fusion.28
  629.7 1.2 convolution_subtract_fusion.1
  630.9 0.4 fusion.42
  631.3 1.3 convolution_subtract_fusion
  632.7 0.4 fusion.40
  633.1 1.6 convolution_subtract_fusion.2
  634.7 0.4 fusion.39
  635.1 1.8 convolution_convert_fusion
  637.0 79.5 %all-gather.2.cloned.1.call-done = bf16[4096,512]{1,0:T(8,128)(2,1)} async-done(((bf16[128,512]{1,0:T(8,128)(2,1)}), bf16[4096,512]{1,0:T(8,128)(2,1)}) %all-gather.2.cloned.1.call-update) | async-done | bytes 4194320 | tf_op jit(solution)/shard_map/all_gather | solution.py:37
  716.5 4.7 fusion.54
  721.2 5.3 all-reduce.11
  726.6 43.1 %all-reduce.10.cloned.1.call-done = bf16[512,256]{1,0:T(8,128)(2,1)} async-done(((bf16[512,256]{1,0:T(8,128)(2,1)}), bf16[512,256]{1,0:T(8,128)(2,1)}) %all-reduce.10.cloned.1.call-update) | async-done | bytes 262160 | tf_op jit(solution)/shard_map/psum | solution.py:43
  769.7 1.1 fusion.18
  770.8 75.1 %psum.39 = f32[512]{0:T(512)S(1)} all-reduce(f32[512]{0:T(512)S(1)} %fusion.18), channel_id=1, replica_groups=mesh['dp'=4,'fsdp'=2,'tp'=32] {'tp'}, use_global_device_ids=true, to_apply=%region_14.15 | all-reduce | flops 512 | bytes 4096 | tf_op jit(solution)/shard_map/psum | solution.py:44
  845.9 1.1 convert_multiply_fusion
  847.0 0.8 copy.8
  847.9 5.0 fusion.2
  852.9 3.3 fusion.1
  (30 shorter events, 0.4 us)
Async XLA Ops:
  7.2 242.1 %reduce-scatter.2.cloned.1.call-start = ((), (), s32[]{:S(2)}) async-start(), calls=%async_computation.1 | async-start | bytes 8650752 | tf_op jit(solution)/shard_map/reduce_scatter | solution.py:26
  17.5 278.4 %all-reduce.6.cloned.1.call-start = ((), (), s32[]{:S(2)}) async-start(), calls=%async_computation.2 | async-start | bytes 262144 | tf_op jit(solution)/shard_map/psum | solution.py:32
  251.0 235.8 %all-reduce.8.cloned.1.call-start = ((), (), s32[]{:S(2)}) async-start(), calls=%async_computation.3 | async-start | bytes 2097152 | tf_op jit(solution)/shard_map/psum | solution.py:33
  298.9 417.5 %all-gather.2.cloned.1.call-start = ((), (), s32[]{:S(2)}) async-start(), calls=%async_computation.4 | async-start | bytes 4325376 | tf_op jit(solution)/shard_map/all_gather | solution.py:37
  573.2 61.9 %copy-start.4 = (bf16[128,512]{1,0:T(8,128)(2,1)S(1)}, bf16[128,512]{1,0:T(8,128)(2,1)}, u32[]{:S(2)}) copy-start(bf16[128,512]{1,0:T(8,128)(2,1)} %all-reduce.6.cloned.1.call-done) | copy-start | bytes 393220
  574.3 142.1 %copy-start.1 = (bf16[1,4096,256]{2,1,0:T(8,128)(2,1)S(1)}, bf16[1,4096,256]{2,1,0:T(8,128)(2,1)}, u32[]{:S(2)}) copy-start(bf16[1,4096,256]{2,1,0:T(8,128)(2,1)} %param.4) | copy-start | bytes 6291460
  636.9 132.7 %all-reduce.10.cloned.1.call-start = ((), (), s32[]{:S(2)}) async-start(), calls=%async_computation.5 | async-start | bytes 524288 | tf_op jit(solution)/shard_map/psum | solution.py:43
  847.8 5.0 copy-start
  847.8 5.1 copy-start.2
  847.8 5.1 copy-start.3
Sparse Core Ops, SparseCore 0:
  17.7 231.6 reduce-scatter.1
  252.3 43.5 all-reduce.5
  300.0 186.7 all-reduce.7
  637.0 79.3 all-gather.1
  726.7 42.9 all-reduce.9
where the time goes:
time: 867 us; the launch traced here: 863 us
  waiting for transfers between devices  586 us (68%)
  other arithmetic  127 us (15%)
  blocking collectives  82.4 us (10%)
  matrix products  33.5 us (4%)
  between operations  16.8 us (2%)
  local copies, waits for them, and re-layouts  16.7 us (2%)
    reduce_scatter x1, waiting for transfers between devices, shards(): lax.psum_scatter(jnp.dot(buffer_low, basis_full, preferred_element_type=j...  232 us
    psum x1, waiting for transfers between devices, shards(): lax.psum(jnp.dot(left_mean.T, left_mean, precision=lax.Precision.HIGHEST)...  186 us
    all_gather x1, waiting for transfers between devices, shards(): ortho_low = lax.all_gather(ortho_share, 'tp', axis=0, tiled=True)  79.5 us
    another operation x14, other arithmetic, orthonormal(): lower = jnp.linalg.cholesky(gram)  78.8 us
    psum x1, blocking collectives, shards(): squares = lax.psum(jnp.sum(right_mean * right_mean, axis=1), 'tp')  75.1 us
    psum x1, waiting for transfers between devices, shards(): lax.psum(share_left.astype(jnp.bfloat16), 'dp').astype(jnp.float32)  44.9 us
    psum x1, waiting for transfers between devices, shards(): lax.psum(summed_right.astype(jnp.bfloat16), 'dp').astype(jnp.float32)  43.1 us
    another operation x3, other arithmetic, orthonormal(): jax.scipy.linalg.solve_triangular(lower, jnp.eye(gram.shape[0], dtype=jnp...  41.2 us
  transfers between devices with their start and end apart: 5, of which 5 were waited for; matrix products, arithmetic and copies ran while one was open for 0% of the time, Pallas kernels for 0%

commit v1 on v0

v1 whole, which is shorter than its diff:
```python
import functools

import jax
import jax.numpy as jnp
from jax import lax
from jax.experimental import pallas as pl
from jax.experimental.pallas import tpu as pltpu
from jax.sharding import PartitionSpec as P

D = 8192
R = 512
NX, NY, NZ = 4, 4, 8
ROWS = 32
LOCAL_ROWS = NX * NY * NZ * ROWS
COLS = 256
MESH = pl.DeviceIdType.MESH
F32, BF16 = jnp.float32, jnp.bfloat16
MIB = 2**20


def place():
    tp = lax.axis_index("tp")
    return lax.axis_index("dp"), lax.axis_index("fsdp"), lax.rem(tp, NY), lax.div(tp, NY)


def x_peer(d):
    p = lax.rem(lax.axis_index("dp") + d, NX)
    return p, {"dp": p}


def y_peer(d):
    _, _, y, z = place()
    p = lax.rem(y + d, NY)
    return p, {"tp": z * NY + p}


def z_peer(d):
    _, _, y, z = place()
    p = lax.rem(z + d, NZ)
    return p, {"tp": p * NY + y}


def pair_peer(d):
    x, c, _, _ = place()
    p = lax.rem(x * 2 + c + d, 2 * NX)
    return p, {"dp": lax.div(p, 2), "fsdp": lax.rem(p, 2)}


SPANS = {"x": (x_peer, NX), "y": (y_peer, NY), "z": (z_peer, NZ), "pair": (pair_peer, 2 * NX)}


def peers(axis):
    find, n = SPANS[axis]
    return [find(d) for d in range(1, n)]


def greet(devices):
    barrier = pltpu.get_barrier_semaphore()
    for device in devices:
        pl.semaphore_signal(barrier, inc=1, device_id=device, device_id_type=MESH)
    pl.semaphore_wait(barrier, len(devices))


class Sender:
    def __init__(self, send, recv):
        self.send, self.recv, self.used = send, recv, 0

    def start(self, src, dst, device):
        k = self.used
        self.used += 1
        copy = pltpu.make_async_remote_copy(
            src_ref=src,
            dst_ref=dst,
            send_sem=self.send.at[k],
            recv_sem=self.recv.at[k],
            device_id=device,
            device_id_type=MESH,
        )
        copy.start()
        return copy


def settle(copies):
    for copy in copies:
        copy.wait()


def front_kernel(
    mom, grad, basis, left, gram, right,
    low, base, part, rx1, ry1, rz1, sx1, sy1, sz1, rx2, ry2, rz2, sx2, sy2, sz2, rx3, ry3, rz3,
    gsend, grecv, tpart, trecv, tsum, send, recv,
):
    x, c, y, z = place()
    sender = Sender(send, recv)
    sibling = {"fsdp": 1 - c}
    every = [p for a in ("x", "y", "z", "pair") for _, p in peers(a)]
    greet(every)

    base[c] = basis[...].astype(BF16)
    basis_copy = sender.start(base.at[c], base.at[c], sibling)

    def lower(i, _):
        rows = pl.ds(pl.multiple_of(i * 256, 256), 256)
        low[rows, :] = (mom[0, rows, :] + grad[0, rows, :].astype(F32)).astype(BF16)
        return 0

    lax.fori_loop(0, LOCAL_ROWS // 256, lower, 0)
    basis_copy.wait()

    def product(i, _):
        rows = pl.ds(pl.multiple_of(i * 256, 256), 256)
        block = low[rows, :]
        xi, yi = lax.div(i, NY), lax.rem(i, NY)
        for h in range(2):
            value = jnp.dot(block, base[h], preferred_element_type=F32).astype(BF16)
            part[xi, yi, :, :, h * 256 : (h + 1) * 256] = value.reshape(NZ, ROWS, 256)
        return 0

    lax.fori_loop(0, NX * NY, product, 0)

    cx, cy, cz = pl.ds(0, 256), pl.ds(256, 128), pl.ds(384, 128)
    px, py, pz = peers("x"), peers("y"), peers("z")

    x1 = [sender.start(part.at[p, :, :, :, cx], rx1.at[k], dev) for k, (p, dev) in enumerate(px)]
    y1 = [sender.start(part.at[:, p, :, :, cy], ry1.at[k], dev) for k, (p, dev) in enumerate(py)]
    z1 = [sender.start(part.at[:, :, p, :, cz], rz1.at[k], dev) for k, (p, dev) in enumerate(pz)]
    settle(x1)
    for i in range(NY):
        total = part[x, i, :, :, 0:256].astype(F32)
        for k in range(NX - 1):
            total = total + rx1[k, i].astype(F32)
        sx1[i] = total.astype(BF16)
    x2 = [sender.start(sx1.at[p], rx2.at[k], dev) for k, (p, dev) in enumerate(py)]
    settle(y1)
    for i in range(NX):
        total = part[i, y, :, :, 256:384].astype(F32)
        for k in range(NY - 1):
            total = total + ry1[k, i].astype(F32)
        sy1[i] = total.astype(BF16)
    y2 = [sender.start(sy1.at[p], ry2.at[k], dev) for k, (p, dev) in enumerate(px)]
    settle(z1)
    for i in range(NX):
        total = part[i, :, z, :, 384:512].astype(F32)
        for k in range(NZ - 1):
            total = total + rz1[k, i].astype(F32)
        sz1[i] = total.astype(BF16)
    z2 = [sender.start(sz1.at[p], rz2.at[k], dev) for k, (p, dev) in enumerate(px)]

    settle(x2)
    total = sx1[y].astype(F32)
    for k in range(NY - 1):
        total = total + rx2[k].astype(F32)
    sx2[...] = total.astype(BF16)
    x3 = [sender.start(sx2.at[p], rx3.at[k], dev) for k, (p, dev) in enumerate(pz)]
    settle(y2)
    total = sy1[x].astype(F32)
    for k in range(NX - 1):
        total = total + ry2[k].astype(F32)
    sy2[...] = total.astype(BF16)
    y3 = [sender.start(sy2.at[p], ry3.at[k], dev) for k, (p, dev) in enumerate(pz)]
    settle(z2)
    total = sz1[x].astype(F32)
    for k in range(NX - 1):
        total = total + rz2[k].astype(F32)
    sz2[...] = total.astype(BF16)
    z3 = [sender.start(sz2.at[p], rz3.at[k], dev) for k, (p, dev) in enumerate(py)]

    settle(x3)
    total = sx2[z].astype(F32)
    for k in range(NZ - 1):
        total = total + rx3[k].astype(F32)
    left[x, y, z, :, 0:256] = (total / NX).astype(BF16)
    mine = left.at[x, y, z, :, cx]
    x4 = [sender.start(mine, mine, dev) for _, dev in pz]
    settle(y3)
    total = sy2[z].astype(F32)
    for k in range(NZ - 1):
        total = total + ry3[k].astype(F32)
    left[x, y, z, :, 256:384] = (total / NX).astype(BF16)
    mine = left.at[x, y, z, :, cy]
    y4 = [sender.start(mine, mine, dev) for _, dev in pz]
    settle(z3)
    total = sz2[y].astype(F32)
    for k in range(NY - 1):
        total = total + rz3[k].astype(F32)
    left[x, y, z, :, 384:512] = (total / NX).astype(BF16)
    mine = left.at[x, y, z, :, cz]
    z4 = [sender.start(mine, mine, dev) for _, dev in py]

    settle(x4)
    mine = left.at[x, y, :, :, cx]
    x5 = [sender.start(mine, mine, dev) for _, dev in py]
    settle(y4)
    mine = left.at[x, y, :, :, cy]
    y5 = [sender.start(mine, mine, dev) for _, dev in px]
    settle(z4)
    mine = left.at[x, :, z, :, cz]
    z5 = [sender.start(mine, mine, dev) for _, dev in px]

    settle(x5)
    mine = left.at[x, :, :, :, cx]
    x6 = [sender.start(mine, mine, dev) for _, dev in px]
    settle(y5)
    mine = left.at[:, y, :, :, cy]
    y6 = [sender.start(mine, mine, dev) for _, dev in py]
    settle(z5)
    mine = left.at[:, :, z, :, cz]
    z6 = [sender.start(mine, mine, dev) for _, dev in pz]
    settle(x6 + y6 + z6)

    gsend[...] = jnp.zeros_like(gsend)
    tpart[...] = jnp.zeros_like(tpart)

    def products(i, _):
        xi, half = lax.div(i, 2), lax.rem(i, 2)
        block = left[xi, pl.ds(half * 2, 2)].reshape(512, R)
        rows = pl.ds(pl.multiple_of(i * 512, 512), 512)
        gsend[...] += lax.dot_general(
            block, block, (((0,), (0,)), ((), ())), preferred_element_type=F32
        )
        tpart[...] += lax.dot_general(
            low[rows, :], block, (((0,), (0,)), ((), ())), preferred_element_type=F32
        ).reshape(tpart.shape)
        return 0

    lax.fori_loop(0, 8, products, 0)
    g1 = sender.start(gsend, grecv, sibling)
    around = peers("pair")
    t1 = [sender.start(tpart.at[p], trecv.at[k], dev) for k, (p, dev) in enumerate(around)]
    settle(t1)
    me = x * 2 + c
    total = tpart[me]
    for k in range(2 * NX - 1):
        total = total + trecv[k]
    right[me] = total / NX
    mine = right.at[me]
    t2 = [sender.start(mine, mine, dev) for _, dev in around]
    g1.wait()
    gram[...] = gsend[...] + grecv[...]
    settle(t2)


def front(momentum, gradient, basis):
    vmem = pl.BlockSpec(memory_space=pltpu.VMEM)
    scratch = [
        pltpu.VMEM((LOCAL_ROWS, COLS), BF16),
        pltpu.VMEM((2, COLS, 256), BF16),
        pltpu.VMEM((NX, NY, NZ, ROWS, R), BF16),
        pltpu.VMEM((3, NY, NZ, ROWS, 256), BF16),
        pltpu.VMEM((3, NX, NZ, ROWS, 128), BF16),
        pltpu.VMEM((7, NX, NY, ROWS, 128), BF16),
        pltpu.VMEM((NY, NZ, ROWS, 256), BF16),
        pltpu.VMEM((NX, NZ, ROWS, 128), BF16),
        pltpu.VMEM((NX, NY, ROWS, 128), BF16),
        pltpu.VMEM((3, NZ, ROWS, 256), BF16),
        pltpu.VMEM((3, NZ, ROWS, 128), BF16),
        pltpu.VMEM((3, NY, ROWS, 128), BF16),
        pltpu.VMEM((NZ, ROWS, 256), BF16),
        pltpu.VMEM((NZ, ROWS, 128), BF16),
        pltpu.VMEM((NY, ROWS, 128), BF16),
        pltpu.VMEM((7, ROWS, 256), BF16),
        pltpu.VMEM((7, ROWS, 128), BF16),
        pltpu.VMEM((3, ROWS, 128), BF16),
        pltpu.VMEM((R, R), F32),
        pltpu.VMEM((R, R), F32),
        pltpu.VMEM((8, 32, R), F32),
        pltpu.VMEM((7, 32, R), F32),
        pltpu.VMEM((32, R), F32),
        pltpu.SemaphoreType.DMA((104,)),
        pltpu.SemaphoreType.DMA((104,)),
    ]
    return pl.pallas_call(
        front_kernel,
        out_shape=(
            jax.ShapeDtypeStruct((NX, NY, NZ, ROWS, R), BF16),
            jax.ShapeDtypeStruct((R, R), F32),
            jax.ShapeDtypeStruct((8, 32, R), F32),
        ),
        in_specs=[vmem] * 3,
        out_specs=(vmem,) * 3,
        scratch_shapes=scratch,
        compiler_params=pltpu.CompilerParams(
            collective_id=0, has_side_effects=True, vmem_limit_bytes=56 * MIB
        ),
        name="front",
    )(momentum, gradient, basis)


def squares_kernel(right, total, own, ry, mid, rz, send, recv):
    sender = Sender(send, recv)
    py, pz = peers("y"), peers("z")
    greet([dev for _, dev in py + pz])
    values = right[...]
    own[...] = jnp.broadcast_to(jnp.sum(values * values, axis=0, keepdims=True), own.shape)
    y1 = [sender.start(own, ry.at[k], dev) for k, (_, dev) in enumerate(py)]
    settle(y1)
    value = own[...]
    for k in range(NY - 1):
        value = value + ry[k]
    mid[...] = value
    z1 = [sender.start(mid, rz.at[k], dev) for k, (_, dev) in enumerate(pz)]
    settle(z1)
    value = mid[...]
    for k in range(NZ - 1):
        value = value + rz[k]
    total[...] = value


def squares_of(right):
    vmem = pl.BlockSpec(memory_space=pltpu.VMEM)
    return pl.pallas_call(
        squares_kernel,
        out_shape=jax.ShapeDtypeStruct((8, R), F32),
        in_specs=[vmem],
        out_specs=vmem,
        scratch_shapes=[
            pltpu.VMEM((8, R), F32),
            pltpu.VMEM((3, 8, R), F32),
            pltpu.VMEM((8, R), F32),
            pltpu.VMEM((7, 8, R), F32),
            pltpu.SemaphoreType.DMA((10,)),
            pltpu.SemaphoreType.DMA((10,)),
        ],
        compiler_params=pltpu.CompilerParams(collective_id=1, has_side_effects=True),
        name="squares",
    )(right)


def finish_kernel(left, high, rest, right, following, mom, grad, new_mom, update):
    block = left[...]
    ortho = (
        jnp.dot(block, high[...], preferred_element_type=F32)
        + jnp.dot(block, rest[...], preferred_element_type=F32)
    ).astype(BF16)
    across = (((1,), (1,)), ((), ()))
    lowrank = lax.dot_general(ortho, right[...], across, preferred_element_type=F32)
    new_mom[0] = mom[0] + grad[0].astype(F32) - 0.05 * lowrank
    factor = D / (R**0.5)
    product = lax.dot_general(ortho, following[...], across, preferred_element_type=F32)
    update[...] = (product * factor).astype(BF16)


def finish(left, high, rest, right, following, momentum, gradient):
    tile = 512
    whole = lambda shape: pl.BlockSpec(shape, lambda i: (0,) * len(shape))
    rows = pl.BlockSpec((tile, R), lambda i: (i, 0))
    cube = pl.BlockSpec((1, tile, COLS), lambda i: (0, i, 0))
    return pl.pallas_call(
        finish_kernel,
        grid=(LOCAL_ROWS // tile,),
        out_shape=(
            jax.ShapeDtypeStruct((1, LOCAL_ROWS, COLS), F32),
            jax.ShapeDtypeStruct((LOCAL_ROWS, COLS), BF16),
        ),
        in_specs=[rows, whole((R, R)), whole((R, R)), whole((COLS, R)), whole((COLS, R)), cube, cube],
        out_specs=(cube, pl.BlockSpec((tile, COLS), lambda i: (i, 0))),
        compiler_params=pltpu.CompilerParams(vmem_limit_bytes=40 * MIB),
        name="finish",
    )(left, high, rest, right, following, momentum, gradient)


def inverse_transposed(gram):
    lower = jnp.linalg.cholesky(gram)
    inverse = jax.scipy.linalg.solve_triangular(lower, jnp.eye(R, dtype=F32), lower=True)
    return inverse.T


def shards(momentum, gradient, basis):
    left, gram, right = front(momentum, gradient, basis)
    upper = inverse_transposed(gram)
    right_mean = jnp.dot(right.reshape(COLS, R), upper, precision=lax.Precision.HIGHEST)
    squares = squares_of(right_mean)[0:1]
    following = right_mean * (1.0 / jnp.sqrt(squares / D + 1e-05))
    new_basis = lax.dynamic_slice_in_dim(following, lax.axis_index("fsdp") * 256, 256, 1)
    high = upper.astype(BF16)
    rest = (upper - high.astype(F32)).astype(BF16)
    new_momentum, update = finish(
        left.reshape(LOCAL_ROWS, R), high, rest, right_mean.astype(BF16),
        following.astype(BF16), momentum, gradient,
    )
    return (new_momentum, new_basis, update)


def solution(mesh):
    in_specs = (P("dp", "fsdp", "tp"), P("dp", "fsdp", "tp"), P("tp", "fsdp"))
    out_specs = (P("dp", "fsdp", "tp"), P("tp", "fsdp"), P("fsdp", "tp"))
    return jax.shard_map(shards, mesh=mesh, in_specs=in_specs, out_specs=out_specs, check_vma=False)
```

time: 867 us -> 296 us (0.34)
  waiting for transfers between devices: 586 us -> 0 us
  Pallas kernels: 0 us -> 136 us
  blocking collectives: 82.4 us -> 0 us
  matrix products: 33.5 us -> 9.11 us
  between operations: 16.8 us -> 3.42 us
    psum x3 -> x0, waiting for transfers between devices: 274 us -> none  [the longest x1 186 us: shards(): lax.psum(jnp.dot(left_mean.T, left_mean, precision=lax.Precision.HIGHEST)...]
    reduce_scatter x1 -> x0, waiting for transfers between devices: 232 us -> none  [shards(): lax.psum_scatter(jnp.dot(buffer_low, basis_full, preferred_element_type=j...]
    pallas_call x0 -> x3, Pallas kernels: none -> 136 us  [the longest x1 112 us: front(): pl.pallas_call(front_kernel, out_shape=(jax.ShapeDtypeStruct((NX, NY, NZ,...]
    psum x2 -> x0, blocking collectives: 80.4 us -> none  [the longest x1 75.1 us: shards(): squares = lax.psum(jnp.sum(right_mean * right_mean, axis=1), 'tp')]
    all_gather x1 -> x0, waiting for transfers between devices: 79.5 us -> none  [shards(): ortho_low = lax.all_gather(ortho_share, 'tp', axis=0, tiled=True)]
    dot_general x6 -> x1, matrix products: 25.2 us -> 3.3 us  [shards(): jnp.dot(right.reshape(COLS, R), upper, precision=lax.Precision.HIGHEST)]
  transfers between devices with their start and end apart: 5 -> 0, of which waited for: 5 -> 0; matrix products, arithmetic and copies ran while one was open for 0% -> 0% of each run, Pallas kernels for 0% -> 0%
where the time goes in v1:
time: 296 us; the launch traced here: 292 us
  Pallas kernels  136 us (46%)
  other arithmetic  126 us (43%)
  local copies, waits for them, and re-layouts  16.7 us (6%)
  matrix products  9.11 us (3%)
  between operations  3.42 us (1%)
    pallas_call x1, Pallas kernels, front(): pl.pallas_call(front_kernel, out_shape=(jax.ShapeDtypeStruct((NX, NY, NZ,...  112 us
    another operation x14, other arithmetic, inverse_transposed(): lower = jnp.linalg.cholesky(gram)  78.8 us
    another operation x3, other arithmetic, inverse_transposed(): jax.scipy.linalg.solve_triangular(lower, jnp.eye(R, dtype=F32), lower=True)  40.3 us
    pallas_call x1, Pallas kernels, squares_of(): pl.pallas_call(squares_kernel, out_shape=jax.ShapeDtypeStruct((8, R), F32...  15.2 us
    another operation x12, local copies, waits for them, and re-layouts  10.3 us
    pallas_call x1, Pallas kernels, finish(): pl.pallas_call(finish_kernel, grid=(LOCAL_ROWS // tile,), out_shape=(jax....  8.81 us

profile of v1, /device:TPU:6, one launch (start us, length us, event | category | flops | bytes accessed | tf_op | source)
XLA Modules:
  0.0 291.6 jit_solution(15928370434506962601)
XLA Ops:
  0.7 0.8 iota_compare_fusion
  1.4 0.1 fusion.10
  1.6 112.2 %front.1 = (bf16[4,4,8,32,512]{4,3,2,1,0:T(8,128)(2,1)}, f32[512,512]{1,0:T(8,128)}, f32[8,32,512]{2,1,0:T(8,128)}) custom-call(f32[1,4096,256]{2,1,0:T(8,128)} %mom.3, bf16[1,4096,256]{2,1,0:T(8,128)(2,1)} %grad.3, f32[256,256]{1,0:T(8,128)} %basis.1), custom_call_target="tpu_custom_call" | custom-call | tf_op jit(solution)/shard_map/front/pallas_call | solution.py:272
  113.7 1.6 copy.6
  115.3 1.4 fusion.1
  116.8 11.7 %cholesky.104 = f32[128,128]{1,0:T(8,128)S(1)} custom-call(f32[128,128]{1,0:T(8,128)S(1)} %cholesky.266), custom_call_target="Cholesky" | custom-call | tf_op jit(solution)/shard_map/jit(cholesky)/cholesky | solution.py:363
  128.5 9.8 %custom-call.31 = f32[1,128,128]{1,2,0:T(8,128)S(1)} custom-call(f32[1,128,128]{2,1,0:T(8,128)S(1)} %get-tuple-element.43), custom_call_target="InvertDiagBlocksLowerTriangular" | custom-call | tf_op jit(solution)/shard_map/jit(cholesky)/cholesky | solution.py:363
  138.3 0.1 cholesky.224
  138.5 0.3 constant_dynamic-update-slice_fusion.3
  138.8 0.3 convolution_subtract_fusion.3
  139.1 11.7 %cholesky.217 = f32[128,128]{1,0:T(8,128)S(1)} custom-call(f32[128,128]{1,0:T(8,128)S(1)} %cholesky.270), custom_call_target="Cholesky" | custom-call | tf_op jit(solution)/shard_map/jit(cholesky)/cholesky | solution.py:363
  150.9 0.7 compare_reduce_fusion.2
  152.8 10.0 %custom-call.32 = f32[1,128,128]{1,2,0:T(8,128)S(1)} custom-call(f32[1,128,128]{2,1,0:T(8,128)S(1)} %get-tuple-element.40), custom_call_target="InvertDiagBlocksLowerTriangular" | custom-call | tf_op jit(solution)/shard_map/jit(cholesky)/cholesky | solution.py:363
  162.8 0.3 convolution_dynamic-update-slice_fusion
  163.0 0.4 convolution_subtract_fusion.4
  163.4 11.7 %cholesky.238 = f32[128,128]{1,0:T(8,128)S(1)} custom-call(f32[128,128]{1,0:T(8,128)S(1)} %cholesky.275), custom_call_target="Cholesky" | custom-call | tf_op jit(solution)/shard_map/jit(cholesky)/cholesky | solution.py:363
  175.2 0.7 compare_reduce_fusion.1
  176.5 9.8 %custom-call.33 = f32[1,128,128]{1,2,0:T(8,128)S(1)} custom-call(f32[1,128,128]{2,1,0:T(8,128)S(1)} %get-tuple-element.37), custom_call_target="InvertDiagBlocksLowerTriangular" | custom-call | tf_op jit(solution)/shard_map/jit(cholesky)/cholesky | solution.py:363
  186.3 0.2 convolution_dynamic-update-slice_fusion.1
  186.5 0.4 convolution_subtract_fusion.5
  186.9 11.9 %cholesky.255 = f32[128,128]{1,0:T(8,128)S(1)} custom-call(f32[128,128]{1,0:T(8,128)S(1)} %convolution_subtract_fusion.5), custom_call_target="Cholesky" | custom-call | tf_op jit(solution)/shard_map/jit(cholesky)/cholesky | solution.py:363
  198.8 0.7 compare_reduce_fusion
  200.1 0.1 select_select_fusion
  200.2 10.3 %while.1 = (s32[]{:T(128)}, f32[512,512]{1,0:T(8,128)S(1)}, s32[4,2]{0,1:T(2,128)S(1)}, f32[4,128,128]{2,1,0:T(8,128)}, s32[]{:T(128)}) while((s32[]{:T(128)}, f32[512,512]{1,0:T(8,128)S(1)}, s32[4,2]{0,1:T(2,128)S(1)}, f32[4,128,128]{2,1,0:T(8,128)}, s32[]{:T(128)}) %tuple.33), condition=%wide.while_cond, body=%wide.while_body.sunk | while | flops 2 | bytes 132205 | solution.py:364
  200.2 0.1 constant_dynamic-slice_fusion.3
  200.3 0.5 fusion.43
  200.9 1.9 bitcast_dynamic-update-slice_fusion.2
  202.8 0.1 constant_dynamic-slice_fusion.3
  202.9 0.5 fusion.43
  203.4 1.9 bitcast_dynamic-update-slice_fusion.2
  205.4 0.1 constant_dynamic-slice_fusion.3
  205.4 0.5 fusion.43
  206.0 1.9 bitcast_dynamic-update-slice_fusion.2
  207.9 0.1 constant_dynamic-slice_fusion.3
  208.0 0.5 fusion.43
  208.6 1.9 bitcast_dynamic-update-slice_fusion.2
  210.5 40.1 %custom-call.34 = f32[4,128,128]{1,2,0:T(8,128)S(1)} custom-call(f32[4,128,128]{2,1,0:T(8,128)} %get-tuple-element.20), custom_call_target="InvertDiagBlocksLowerTriangular" | custom-call | tf_op jit(solution)/shard_map/jit(_solve_triangular)/triangular_solve | solution.py:364
  250.6 1.1 fusion.12
  251.7 0.8 copy.7
  252.6 0.4 convolution_subtract_fusion.1
  252.9 0.4 fusion.25
  253.4 0.8 copy.8
  254.2 0.4 convolution_subtract_fusion
  254.6 0.4 fusion.23
  255.1 0.6 convolution_subtract_fusion.2
  255.7 0.6 fusion.22
  256.3 0.0 copy-start.3
  256.3 0.0 copy-start.1
  256.3 0.1 copy.9
  256.5 0.0 copy-start.4
  256.5 3.3 %fusion.18.right = f32[256,512]{1,0:T(8,128)} fusion(f32[256,512]{1,0:T(8,128)} %bitcast.61, f32[128,512]{0,1:T(8,128)S(1)} %fusion.22, f32[128,512]{0,1:T(8,128)S(1)} %copy.9, f32[128,512]{0,1:T(8,128)} %copy.8, f32[128,512]{0,1:T(8,128)} %copy.7), kind=kOutput, calls=%fused_computation.36 | convolution fusion | flops 806092800 | bytes 2097152 | tf_op jit(solution)/shard_map/dot_general | solution.py:371
  259.8 15.2 %squares.1 = f32[8,512]{1,0:T(8,128)} custom-call(f32[256,512]{1,0:T(8,128)} %fusion.18.right), custom_call_target="tpu_custom_call" | custom-call | tf_op jit(solution)/shard_map/squares/pallas_call | solution.py:311
  274.9 0.0 copy-start
  275.0 0.9 add_rsqrt_fusion
  275.8 0.0 copy-done.3
  275.8 0.0 copy-done.4
  275.8 1.5 fusion.34
  277.4 0.7 constant_dynamic-slice_fusion.1
  278.1 1.2 fusion.rest
  279.3 1.2 bitcast_convert_fusion.high
  280.6 0.0 copy-done.1
  280.6 0.0 copy-done
  280.6 2.2 copy-done.2
  282.8 8.8 %finish.1 = (f32[1,4096,256]{2,1,0:T(8,128)}, bf16[4096,256]{1,0:T(8,128)(2,1)}) custom-call(bf16[4096,512]{1,0:T(8,128)(2,1)S(1)} %bitcast.59, bf16[512,512]{1,0:T(8,128)(2,1)S(1)} %bitcast_convert_fusion.high, bf16[512,512]{1,0:T(8,128)(2,1)S(1)} %fusion.rest, bf16[256,512]{1,0:T(8,128)(2,1)S(1)} %get-tuple-element.33.right, ...), custom_call_target="tpu_custom_call" | custom-call | tf_op jit(solution)/shard_map/finish/pallas_call | solution.py:348
  (11 shorter events, 0.2 us)
Async XLA Ops:
  256.3 19.5 %copy-start.3 = (f32[128,512]{0,1:T(8,128)}, f32[128,512]{0,1:T(8,128)S(1)}, u32[]{:S(2)}) copy-start(f32[128,512]{0,1:T(8,128)S(1)} %fusion.22) | copy-start | bytes 786436
  256.3 24.3 %copy-start.1 = (bf16[1,4096,256]{2,1,0:T(8,128)(2,1)S(1)}, bf16[1,4096,256]{2,1,0:T(8,128)(2,1)}, u32[]{:S(2)}) copy-start(bf16[1,4096,256]{2,1,0:T(8,128)(2,1)} %grad.3) | copy-start | bytes 6291460
  256.5 19.4 %copy-start.4 = (f32[128,512]{0,1:T(8,128)}, f32[128,512]{0,1:T(8,128)S(1)}, u32[]{:S(2)}) copy-start(f32[128,512]{0,1:T(8,128)S(1)} %copy.9) | copy-start | bytes 786436
  274.9 5.7 %copy-start = (f32[1,4096,256]{2,1,0:T(8,128)S(1)}, f32[1,4096,256]{2,1,0:T(8,128)}, u32[]{:S(2)}) copy-start(f32[1,4096,256]{2,1,0:T(8,128)} %mom.3) | copy-start | bytes 12582916
  280.6 2.2 copy-start.2

commit v2 on v1

--- a/solution.py
+++ b/solution.py
@@ -1,5 +1,3 @@
-import functools
-
 import jax
 import jax.numpy as jnp
 from jax import lax
@@ -15,6 +13,7 @@
 COLS = 256
 MESH = pl.DeviceIdType.MESH
 F32, BF16 = jnp.float32, jnp.bfloat16
+HIGH = lax.Precision.HIGHEST
 MIB = 2**20
 
 
@@ -65,10 +64,10 @@
     def __init__(self, send, recv):
         self.send, self.recv, self.used = send, recv, 0
 
-    def start(self, src, dst, device):
+    def make(self, src, dst, device):
         k = self.used
         self.used += 1
-        copy = pltpu.make_async_remote_copy(
+        return pltpu.make_async_remote_copy(
             src_ref=src,
             dst_ref=dst,
             send_sem=self.send.at[k],
@@ -76,6 +75,9 @@
             device_id=device,
             device_id_type=MESH,
         )
+
+    def start(self, src, dst, device):
+        copy = self.make(src, dst, device)
         copy.start()
         return copy
 
@@ -85,10 +87,100 @@
         copy.wait()
 
 
+def splat_rows(v, i):
+    return jnp.broadcast_to(v[i:i+1,:], (8,128))
+
+def diag_inverse(load):
+    n=16
+    sub=lax.broadcasted_iota(jnp.int32,(8,128),0)
+    lane=lax.broadcasted_iota(jnp.int32,(8,128),1)
+    G=[load(g) for g in range(n)]
+    Y=[(lane==sub+8*g).astype(F32) for g in range(n)]
+    out=[]
+    for p in range(n):
+        at=8*p
+        C=[jnp.broadcast_to(G[p][:,at+k:at+k+1],(8,128)) for k in range(8)]
+        c={(i,k): splat_rows(C[k],i) for k in range(8) for i in range(k,8)}
+        r=[None]*8; l={}
+        for j in range(8):
+            piv=c[j,j]
+            rr=lax.rsqrt(piv)
+            rr=rr*(1.5-0.5*piv*rr*rr)
+            r[j]=rr
+            for i in range(j+1,8): l[i,j]=c[i,j]*rr
+            for k in range(j+1,8):
+                for i in range(k,8):
+                    c[i,k]=c[i,k]-l[i,j]*l[k,j]
+        us,ys=[],[]
+        g0,y0=G[p],Y[p]
+        done_y=jnp.zeros((8,128),F32)
+        Lc=[]
+        for j in range(8):
+            col=C[j]
+            for i in range(j): col=col-Lc[i]*l[j,i]
+            col=col*r[j]
+            Lc.append(col)
+            u=splat_rows(g0,j)*r[j]
+            yv=splat_rows(y0,j)*r[j]
+            us.append(u); ys.append(yv)
+            m=jnp.where(sub>j,col,0.0)
+            g0=g0-m*u
+            y0=y0-m*yv
+            done_y=jnp.where(sub==j,yv,done_y)
+        out.append(done_y)
+        for g in range(p+1,n):
+            Cg=[jnp.broadcast_to(G[g][:,at+k:at+k+1],(8,128)) for k in range(8)]
+            L=[]
+            gg,yy=G[g],Y[g]
+            for j in range(8):
+                col=Cg[j]
+                for i in range(j): col=col-L[i]*l[j,i]
+                col=col*r[j]; L.append(col)
+                gg=gg-col*us[j]
+                yy=yy-col*ys[j]
+            G[g],Y[g]=gg,yy
+    return out
+
+def nt(a, b, precision=HIGH):
+    return lax.dot_general(
+        a, b, (((1,), (1,)), ((), ())), precision=precision, preferred_element_type=F32
+    )
+
+
+def nn(a, b):
+    return jnp.dot(a, b, precision=HIGH, preferred_element_type=F32)
+
+def inverse_factor(a, out, between):
+    out[...] = jnp.zeros_like(out)
+
+    def step(kb, _):
+        between(kb)
+        base = pl.multiple_of(kb * 128, 128)
+        rows = diag_inverse(lambda g: a[pl.ds(base + 8 * g, 8), pl.ds(base, 128)])
+        for g in range(16):
+            out[pl.ds(base + 8 * g, 8), pl.ds(base, 128)] = rows[g]
+        for s in range(4):
+
+            @pl.when(kb == s)
+            def _():
+                lo, hi = s * 128, (s + 1) * 128
+                block = out[lo:hi, lo:hi]
+                if s > 0:
+                    out[lo:hi, 0:lo] = nn(block, out[lo:hi, 0:lo])
+                if s < 3:
+                    panel = nt(a[hi:R, lo:hi], block)
+                    a[hi:R, hi:R] = a[hi:R, hi:R] - nt(panel, panel)
+                    out[hi:R, 0:hi] = out[hi:R, 0:hi] - nn(panel, out[lo:hi, 0:hi])
+
+        return 0
+
+    lax.fori_loop(0, 4, step, 0)
+
+
 def front_kernel(
-    mom, grad, basis, left, gram, right,
+    mom, grad, basis, left, right_low, next_low, new_basis,
     low, base, part, rx1, ry1, rz1, sx1, sy1, sz1, rx2, ry2, rz2, sx2, sy2, sz2, rx3, ry3, rz3,
-    gsend, grecv, tpart, trecv, tsum, send, recv,
+    gsend, grecv, tpart, trecv, right, inverse, following, own, ry, mid, rz, send, recv,
 ):
     x, c, y, z = place()
     sender = Sender(send, recv)
@@ -227,17 +319,62 @@
     g1 = sender.start(gsend, grecv, sibling)
     around = peers("pair")
     t1 = [sender.start(tpart.at[p], trecv.at[k], dev) for k, (p, dev) in enumerate(around)]
-    settle(t1)
     me = x * 2 + c
-    total = tpart[me]
-    for k in range(2 * NX - 1):
-        total = total + trecv[k]
-    right[me] = total / NX
     mine = right.at[me]
-    t2 = [sender.start(mine, mine, dev) for _, dev in around]
+    t2 = [sender.make(mine, mine, dev) for _, dev in around]
     g1.wait()
-    gram[...] = gsend[...] + grecv[...]
+    gsend[...] = gsend[...] + grecv[...]
+
+    def between(kb):
+        @pl.when(kb == 2)
+        def _():
+            settle(t1)
+            total = tpart[me]
+            for k in range(2 * NX - 1):
+                total = total + trecv[k]
+            right[me] = total / NX
+            for copy in t2:
+                copy.start()
+
+    inverse_factor(gsend, inverse, between)
+    grecv[...] = inverse[...] - inverse[...].astype(BF16).astype(F32)
     settle(t2)
+
+    mean = nt(right[...].reshape(COLS, R), inverse[...])
+    right_low[...] = mean.astype(BF16)
+    following[...] = mean
+    own[...] = jnp.broadcast_to(jnp.sum(mean * mean, axis=0, keepdims=True), own.shape)
+    y7 = [sender.start(own, ry.at[k], dev) for k, (_, dev) in enumerate(py)]
+
+    def ortho(i, _):
+        xi, yi = lax.div(i, NY), lax.rem(i, NY)
+        block = left[xi, yi].reshape(NZ * ROWS, R)
+        high = inverse[...].astype(BF16)
+        rest = grecv[...].astype(BF16)
+        value = nt(block, high, None) + nt(block, rest, None)
+        left[xi, yi] = value.astype(BF16).reshape(NZ, ROWS, R)
+        return 0
+
+    lax.fori_loop(0, NX * NY // 2, ortho, 0)
+    settle(y7)
+    value = own[...]
+    for k in range(NY - 1):
+        value = value + ry[k]
+    mid[...] = value
+    z7 = [sender.start(mid, rz.at[k], dev) for k, (_, dev) in enumerate(pz)]
+    lax.fori_loop(NX * NY // 2, NX * NY, ortho, 0)
+    settle(z7)
+    value = mid[...]
+    for k in range(NZ - 1):
+        value = value + rz[k]
+    scale = 1.0 / jnp.sqrt(value[0:1] / D + 1e-05)
+    following[...] = following[...] * scale
+    next_low[...] = following[...].astype(BF16)
+    for core in range(2):
+
+        @pl.when(c == core)
+        def _():
+            new_basis[...] = following[:, core * 256 : (core + 1) * 256]
 
 
 def front(momentum, gradient, basis):
@@ -265,19 +402,26 @@
         pltpu.VMEM((R, R), F32),
         pltpu.VMEM((8, 32, R), F32),
         pltpu.VMEM((7, 32, R), F32),
-        pltpu.VMEM((32, R), F32),
-        pltpu.SemaphoreType.DMA((104,)),
-        pltpu.SemaphoreType.DMA((104,)),
+        pltpu.VMEM((8, 32, R), F32),
+        pltpu.VMEM((R, R), F32),
+        pltpu.VMEM((COLS, R), F32),
+        pltpu.VMEM((8, R), F32),
+        pltpu.VMEM((3, 8, R), F32),
+        pltpu.VMEM((8, R), F32),
+        pltpu.VMEM((7, 8, R), F32),
+        pltpu.SemaphoreType.DMA((112,)),
+        pltpu.SemaphoreType.DMA((112,)),
     ]
     return pl.pallas_call(
         front_kernel,
         out_shape=(
             jax.ShapeDtypeStruct((NX, NY, NZ, ROWS, R), BF16),
-            jax.ShapeDtypeStruct((R, R), F32),
-            jax.ShapeDtypeStruct((8, 32, R), F32),
+            jax.ShapeDtypeStruct((COLS, R), BF16),
+            jax.ShapeDtypeStruct((COLS, R), BF16),
+            jax.ShapeDtypeStruct((COLS, 256), F32),
         ),
         in_specs=[vmem] * 3,
-        out_specs=(vmem,) * 3,
+        out_specs=(vmem,) * 4,
         scratch_shapes=scratch,
         compiler_params=pltpu.CompilerParams(
             collective_id=0, has_side_effects=True, vmem_limit_bytes=56 * MIB
@@ -286,52 +430,8 @@
     )(momentum, gradient, basis)
 
 
-def squares_kernel(right, total, own, ry, mid, rz, send, recv):
-    sender = Sender(send, recv)
-    py, pz = peers("y"), peers("z")
-    greet([dev for _, dev in py + pz])
-    values = right[...]
-    own[...] = jnp.broadcast_to(jnp.sum(values * values, axis=0, keepdims=True), own.shape)
-    y1 = [sender.start(own, ry.at[k], dev) for k, (_, dev) in enumerate(py)]
-    settle(y1)
-    value = own[...]
-    for k in range(NY - 1):
-        value = value + ry[k]
-    mid[...] = value
-    z1 = [sender.start(mid, rz.at[k], dev) for k, (_, dev) in enumerate(pz)]
-    settle(z1)
-    value = mid[...]
-    for k in range(NZ - 1):
-        value = value + rz[k]
-    total[...] = value
-
-
-def squares_of(right):
-    vmem = pl.BlockSpec(memory_space=pltpu.VMEM)
-    return pl.pallas_call(
-        squares_kernel,
-        out_shape=jax.ShapeDtypeStruct((8, R), F32),
-        in_specs=[vmem],
-        out_specs=vmem,
-        scratch_shapes=[
-            pltpu.VMEM((8, R), F32),
-            pltpu.VMEM((3, 8, R), F32),
-            pltpu.VMEM((8, R), F32),
-            pltpu.VMEM((7, 8, R), F32),
-            pltpu.SemaphoreType.DMA((10,)),
-            pltpu.SemaphoreType.DMA((10,)),
-        ],
-        compiler_params=pltpu.CompilerParams(collective_id=1, has_side_effects=True),
-        name="squares",
-    )(right)
-
-
-def finish_kernel(left, high, rest, right, following, mom, grad, new_mom, update):
-    block = left[...]
-    ortho = (
-        jnp.dot(block, high[...], preferred_element_type=F32)
-        + jnp.dot(block, rest[...], preferred_element_type=F32)
-    ).astype(BF16)
+def finish_kernel(left, right, following, mom, grad, new_mom, update):
+    ortho = left[...]
     across = (((1,), (1,)), ((), ()))
     lowrank = lax.dot_general(ortho, right[...], across, preferred_element_type=F32)
     new_mom[0] = mom[0] + grad[0].astype(F32) - 0.05 * lowrank
@@ -340,7 +440,7 @@
     update[...] = (product * factor).astype(BF16)
 
 
-def finish(left, high, rest, right, following, momentum, gradient):
+def finish(left, right, following, momentum, gradient):
     tile = 512
     whole = lambda shape: pl.BlockSpec(shape, lambda i: (0,) * len(shape))
     rows = pl.BlockSpec((tile, R), lambda i: (i, 0))
@@ -352,31 +452,17 @@
             jax.ShapeDtypeStruct((1, LOCAL_ROWS, COLS), F32),
             jax.ShapeDtypeStruct((LOCAL_ROWS, COLS), BF16),
         ),
-        in_specs=[rows, whole((R, R)), whole((R, R)), whole((COLS, R)), whole((COLS, R)), cube, cube],
+        in_specs=[rows, whole((COLS, R)), whole((COLS, R)), cube, cube],
         out_specs=(cube, pl.BlockSpec((tile, COLS), lambda i: (i, 0))),
         compiler_params=pltpu.CompilerParams(vmem_limit_bytes=40 * MIB),
         name="finish",
-    )(left, high, rest, right, following, momentum, gradient)
-
-
-def inverse_transposed(gram):
-    lower = jnp.linalg.cholesky(gram)
-    inverse = jax.scipy.linalg.solve_triangular(lower, jnp.eye(R, dtype=F32), lower=True)
-    return inverse.T
+    )(left, right, following, momentum, gradient)
 
 
 def shards(momentum, gradient, basis):
-    left, gram, right = front(momentum, gradient, basis)
-    upper = inverse_transposed(gram)
-    right_mean = jnp.dot(right.reshape(COLS, R), upper, precision=lax.Precision.HIGHEST)
-    squares = squares_of(right_mean)[0:1]
-    following = right_mean * (1.0 / jnp.sqrt(squares / D + 1e-05))
-    new_basis = lax.dynamic_slice_in_dim(following, lax.axis_index("fsdp") * 256, 256, 1)
-    high = upper.astype(BF16)
-    rest = (upper - high.astype(F32)).astype(BF16)
+    ortho, right, following, new_basis = front(momentum, gradient, basis)
     new_momentum, update = finish(
-        left.reshape(LOCAL_ROWS, R), high, rest, right_mean.astype(BF16),
-        following.astype(BF16), momentum, gradient,
+        ortho.reshape(LOCAL_ROWS, R), right, following, momentum, gradient
     )
     return (new_momentum, new_basis, update)
 

time: 296 us -> 149 us (0.50)
  other arithmetic: 126 us -> 0 us
  local copies, waits for them, and re-layouts: 16.7 us -> 4.79 us
  matrix products: 9.11 us -> 0 us
  Pallas kernels: 136 us -> 141 us
    another operation x17 -> x0, other arithmetic: 119 us -> none  [the longest x14 78.8 us: inverse_transposed(): lower = jnp.linalg.cholesky(gram)]
    pallas_call x1, Pallas kernels: 112 us -> 135 us  [front(): pl.pallas_call(front_kernel, out_shape=(jax.ShapeDtypeStruct((NX, NY, NZ,...]
    pallas_call x1 -> x0, Pallas kernels: 15.2 us -> none  [squares_of(): pl.pallas_call(squares_kernel, out_shape=jax.ShapeDtypeStruct((8, R), F32...]
    another operation x20 -> x0, local copies, waits for them, and re-layouts: 12.2 us -> none
    another operation x13 -> x0, matrix products: 5.8 us -> none  [the longest x7 3.93 us: inverse_transposed(): jax.scipy.linalg.solve_triangular(lower, jnp.eye(R, dtype=F32), lower=True)]
    convert_element_type x4 -> x0, other arithmetic: 4.11 us -> none  [the longest x1 1.51 us: shards(): following.astype(BF16)]
    dot_general x1 -> x0, matrix products: 3.3 us -> none  [shards(): jnp.dot(right.reshape(COLS, R), upper, precision=lax.Precision.HIGHEST)]
    pallas_call x1, Pallas kernels: 8.81 us -> 5.84 us  [finish(): pl.pallas_call(finish_kernel, grid=(LOCAL_ROWS // tile,), out_shape=(jax....]
where the time goes in v2:
time: 149 us; the launch traced here: 147 us
  Pallas kernels  141 us (95%)
  local copies, waits for them, and re-layouts  4.79 us (3%)
    pallas_call x1, Pallas kernels, front(): pl.pallas_call(front_kernel, out_shape=(jax.ShapeDtypeStruct((NX, NY, NZ,...  135 us
    pallas_call x1, Pallas kernels, finish(): pl.pallas_call(finish_kernel, grid=(LOCAL_ROWS // tile,), out_shape=(jax....  5.84 us
    unnamed x13, local copies, waits for them, and re-layouts  4.79 us

profile of v2, /device:TPU:6, one launch (start us, length us, event | category | flops | bytes accessed | tf_op | source)
XLA Modules:
  0.0 146.8 jit_solution(13935259936145945209)
XLA Ops:
  0.6 0.0 copy-start.1
  0.6 0.0 copy-start
  0.7 135.5 %front.1 = (bf16[4,4,8,32,512]{4,3,2,1,0:T(8,128)(2,1)}, bf16[256,512]{1,0:T(8,128)(2,1)}, bf16[256,512]{1,0:T(8,128)(2,1)}, f32[256,256]{1,0:T(8,128)}) custom-call(f32[1,4096,256]{2,1,0:T(8,128)} %mom.3, bf16[1,4096,256]{2,1,0:T(8,128)(2,1)} %grad.3, f32[256,256]{1,0:T(8,128)} %basis.1), custom_call_target="tpu_custom_call" | custom-call | tf_op jit(solution)/shard_map/front/pallas_call | solution.py:415
  136.1 0.0 copy-done.1
  136.1 0.0 copy-done
  136.1 0.0 copy-start.2
  136.1 2.2 %copy-done.2 = bf16[4,4,8,32,512]{4,3,2,1,0:T(8,128)(2,1)S(1)} copy-done((bf16[4,4,8,32,512]{4,3,2,1,0:T(8,128)(2,1)S(1)}, bf16[4,4,8,32,512]{4,3,2,1,0:T(8,128)(2,1)}, u32[]{:S(2)}) %copy-start.2) | copy-done | bytes 4194328
  138.3 0.0 copy-start.3
  138.3 0.9 copy-done.3
  139.3 0.0 copy-start.4
  139.3 0.9 copy-done.4
  140.2 0.0 copy-start.5
  140.2 5.8 %finish.1 = (f32[1,4096,256]{2,1,0:T(8,128)}, bf16[4096,256]{1,0:T(8,128)(2,1)}) custom-call(bf16[4096,512]{1,0:T(8,128)(2,1)S(1)} %bitcast.1, bf16[256,512]{1,0:T(8,128)(2,1)S(1)} %copy-done.3, bf16[256,512]{1,0:T(8,128)(2,1)S(1)} %copy-done.4, f32[1,4096,256]{2,1,0:T(8,128)S(1)} %copy-done, bf16[1,4096,256]{2,1,0:T(8,128)(2,1)S(1)} %copy-done.1), custom_call_target="tpu_custom_call" | custom-call | tf_op jit(solution)/shard_map/finish/pallas_call | solution.py:448
  146.1 0.0 copy-done.5
  146.1 0.7 copy.7
Async XLA Ops:
  0.6 135.5 %copy-start.1 = (bf16[1,4096,256]{2,1,0:T(8,128)(2,1)S(1)}, bf16[1,4096,256]{2,1,0:T(8,128)(2,1)}, u32[]{:S(2)}) copy-start(bf16[1,4096,256]{2,1,0:T(8,128)(2,1)} %grad.3) | copy-start | bytes 6291460
  0.6 135.5 %copy-start = (f32[1,4096,256]{2,1,0:T(8,128)S(1)}, f32[1,4096,256]{2,1,0:T(8,128)}, u32[]{:S(2)}) copy-start(f32[1,4096,256]{2,1,0:T(8,128)} %mom.3) | copy-start | bytes 12582916
  136.1 2.2 %copy-start.2 = (bf16[4,4,8,32,512]{4,3,2,1,0:T(8,128)(2,1)S(1)}, bf16[4,4,8,32,512]{4,3,2,1,0:T(8,128)(2,1)}, u32[]{:S(2)}) copy-start(bf16[4,4,8,32,512]{4,3,2,1,0:T(8,128)(2,1)} %get-tuple-element.9) | copy-start | bytes 12582916
  138.3 0.9 copy-start.3
  139.3 0.9 copy-start.4
  140.2 5.8 %copy-start.5 = (f32[256,256]{1,0:T(8,128)S(1)}, f32[256,256]{1,0:T(8,128)}, u32[]{:S(2)}) copy-start(f32[256,256]{1,0:T(8,128)} %get-tuple-element.19) | copy-start | bytes 786436

commit v3 on v2

--- a/solution.py
+++ b/solution.py
@@ -11,6 +11,7 @@
 ROWS = 32
 LOCAL_ROWS = NX * NY * NZ * ROWS
 COLS = 256
+WIDE = 384
 MESH = pl.DeviceIdType.MESH
 F32, BF16 = jnp.float32, jnp.bfloat16
 HIGH = lax.Precision.HIGHEST
@@ -51,13 +52,6 @@
 def peers(axis):
     find, n = SPANS[axis]
     return [find(d) for d in range(1, n)]
-
-
-def greet(devices):
-    barrier = pltpu.get_barrier_semaphore()
-    for device in devices:
-        pl.semaphore_signal(barrier, inc=1, device_id=device, device_id_type=MESH)
-    pl.semaphore_wait(barrier, len(devices))
 
 
 class Sender:
@@ -178,63 +172,94 @@
 
 
 def front_kernel(
-    mom, grad, basis, left, right_low, next_low, new_basis,
-    low, base, part, rx1, ry1, rz1, sx1, sy1, sz1, rx2, ry2, rz2, sx2, sy2, sz2, rx3, ry3, rz3,
-    gsend, grecv, tpart, trecv, right, inverse, following, own, ry, mid, rz, send, recv,
+    momentum, gradient, basis, left, right_low, next_low, new_basis,
+    mom, grad, low, base, part, rx1, ry1, za, zb, zh, zs, sx1, sy1, sz1, rx2, ry2, rz2, sx2, sy2, sz2,
+    rx3, ry3, rz3, gsend, grecv, tpart, trecv, right, inverse, following, own, ry, mid, rz,
+    load, send, recv,
 ):
     x, c, y, z = place()
     sender = Sender(send, recv)
     sibling = {"fsdp": 1 - c}
-    every = [p for a in ("x", "y", "z", "pair") for _, p in peers(a)]
-    greet(every)
-
+    px, py, pz, around = peers("x"), peers("y"), peers("z"), peers("pair")
+    barrier = pltpu.get_barrier_semaphore()
+    greeted = [dev for _, dev in px + py + pz + around]
+    for dev in greeted:
+        pl.semaphore_signal(barrier, inc=1, device_id=dev, device_id_type=MESH)
+
+    order = [p for p, _ in px] + [x]
+    loads = []
+    for k, p in enumerate(order):
+        rows = pl.ds(pl.multiple_of(p * 1024, 1024), 1024)
+        one = pltpu.make_async_copy(momentum.at[0, rows, :], mom.at[p], load.at[2 * k])
+        two = pltpu.make_async_copy(gradient.at[0, rows, :], grad.at[p], load.at[2 * k + 1])
+        one.start()
+        two.start()
+        loads.append((one, two))
     base[c] = basis[...].astype(BF16)
+    pl.semaphore_wait(barrier, len(greeted))
     basis_copy = sender.start(base.at[c], base.at[c], sibling)
 
-    def lower(i, _):
-        rows = pl.ds(pl.multiple_of(i * 256, 256), 256)
-        low[rows, :] = (mom[0, rows, :] + grad[0, rows, :].astype(F32)).astype(BF16)
-        return 0
-
-    lax.fori_loop(0, LOCAL_ROWS // 256, lower, 0)
-    basis_copy.wait()
-
-    def product(i, _):
-        rows = pl.ds(pl.multiple_of(i * 256, 256), 256)
-        block = low[rows, :]
-        xi, yi = lax.div(i, NY), lax.rem(i, NY)
+    top, low16 = pl.ds(0, 16), pl.ds(16, 16)
+    wide, narrow = pl.ds(0, WIDE), pl.ds(WIDE, R - WIDE)
+    x1 = []
+    for k, p in enumerate(order):
+        for copy in loads[k]:
+            copy.wait()
+        low[p] = (mom[p] + grad[p].astype(F32)).astype(BF16)
+        if k == 0:
+            basis_copy.wait()
         for h in range(2):
-            value = jnp.dot(block, base[h], preferred_element_type=F32).astype(BF16)
-            part[xi, yi, :, :, h * 256 : (h + 1) * 256] = value.reshape(NZ, ROWS, 256)
-        return 0
-
-    lax.fori_loop(0, NX * NY, product, 0)
-
-    cx, cy, cz = pl.ds(0, 256), pl.ds(256, 128), pl.ds(384, 128)
-    px, py, pz = peers("x"), peers("y"), peers("z")
-
-    x1 = [sender.start(part.at[p, :, :, :, cx], rx1.at[k], dev) for k, (p, dev) in enumerate(px)]
-    y1 = [sender.start(part.at[:, p, :, :, cy], ry1.at[k], dev) for k, (p, dev) in enumerate(py)]
-    z1 = [sender.start(part.at[:, :, p, :, cz], rz1.at[k], dev) for k, (p, dev) in enumerate(pz)]
+            value = jnp.dot(low[p], base[h], preferred_element_type=F32).astype(BF16)
+            part[p, :, :, :, h * 256 : (h + 1) * 256] = value.reshape(NY, NZ, ROWS, 256)
+        if k < NX - 1:
+            dev = px[k][1]
+            x1.append(sender.start(part.at[p, :, :, top, wide], rx1.at[k], dev))
+
+    def on_z(d):
+        p = lax.rem(z + d + NZ, NZ)
+        return p, {"tp": p * NY + y}
+
+    y1 = [sender.start(part.at[:, p, :, low16, wide], ry1.at[k], dev) for k, (p, dev) in enumerate(py)]
+    halves = (pl.ds(0, 2), pl.ds(2, 2))
+    far, _ = on_z(4)
+    z1 = []
+    for k, d in enumerate((-1, 1)):
+        third, _ = on_z(3 * d)
+        z1.append(sender.start(part.at[:, :, third, :, narrow], za.at[k], on_z(d)[1]))
+    for k, d in enumerate((-1, 1)):
+        z1.append(sender.start(part.at[halves[k], :, far, :, narrow], zh.at[k], on_z(2 * d)[1]))
+    zb1 = []
+    for k, d in enumerate((-1, 1)):
+        near, dev = on_z(d)
+        zb1.append(sender.start(part.at[:, :, near, :, narrow], zb.at[k], dev))
+    settle(z1)
+    for k, d in enumerate((-1, 1)):
+        second, dev = on_z(2 * d)
+        for i in range(NX):
+            total = part[i, :, second, :, WIDE:R].astype(F32) + za[k, i].astype(F32)
+            if i // 2 == k:
+                total = total + zh[k, i % 2].astype(F32)
+            zs[k, i] = total.astype(BF16)
+        zb1.append(sender.start(zs.at[k], zb.at[2 + k], dev))
     settle(x1)
     for i in range(NY):
-        total = part[x, i, :, :, 0:256].astype(F32)
+        total = part[x, i, :, 0:16, 0:WIDE].astype(F32)
         for k in range(NX - 1):
             total = total + rx1[k, i].astype(F32)
         sx1[i] = total.astype(BF16)
     x2 = [sender.start(sx1.at[p], rx2.at[k], dev) for k, (p, dev) in enumerate(py)]
     settle(y1)
     for i in range(NX):
-        total = part[i, y, :, :, 256:384].astype(F32)
+        total = part[i, y, :, 16:32, 0:WIDE].astype(F32)
         for k in range(NY - 1):
             total = total + ry1[k, i].astype(F32)
         sy1[i] = total.astype(BF16)
     y2 = [sender.start(sy1.at[p], ry2.at[k], dev) for k, (p, dev) in enumerate(px)]
-    settle(z1)
+    settle(zb1)
     for i in range(NX):
-        total = part[i, :, z, :, 384:512].astype(F32)
-        for k in range(NZ - 1):
-            total = total + rz1[k, i].astype(F32)
+        total = part[i, :, z, :, WIDE:R].astype(F32)
+        for k in range(4):
+            total = total + zb[k, i].astype(F32)
         sz1[i] = total.astype(BF16)
     z2 = [sender.start(sz1.at[p], rz2.at[k], dev) for k, (p, dev) in enumerate(px)]
 
@@ -261,63 +286,68 @@
     total = sx2[z].astype(F32)
     for k in range(NZ - 1):
         total = total + rx3[k].astype(F32)
-    left[x, y, z, :, 0:256] = (total / NX).astype(BF16)
-    mine = left.at[x, y, z, :, cx]
+    left[x, y, z, 0:16, 0:WIDE] = (total / NX).astype(BF16)
+    mine = left.at[x, y, z, top, wide]
     x4 = [sender.start(mine, mine, dev) for _, dev in pz]
     settle(y3)
     total = sy2[z].astype(F32)
     for k in range(NZ - 1):
         total = total + ry3[k].astype(F32)
-    left[x, y, z, :, 256:384] = (total / NX).astype(BF16)
-    mine = left.at[x, y, z, :, cy]
+    left[x, y, z, 16:32, 0:WIDE] = (total / NX).astype(BF16)
+    mine = left.at[x, y, z, low16, wide]
     y4 = [sender.start(mine, mine, dev) for _, dev in pz]
     settle(z3)
     total = sz2[y].astype(F32)
     for k in range(NY - 1):
         total = total + rz3[k].astype(F32)
-    left[x, y, z, :, 384:512] = (total / NX).astype(BF16)
-    mine = left.at[x, y, z, :, cz]
+    left[x, y, z, :, WIDE:R] = (total / NX).astype(BF16)
+    mine = left.at[x, y, z, :, narrow]
     z4 = [sender.start(mine, mine, dev) for _, dev in py]
 
+    settle(z4)
+    mine = left.at[x, :, z, :, narrow]
+    z5 = [sender.start(mine, mine, dev) for _, dev in px]
     settle(x4)
-    mine = left.at[x, y, :, :, cx]
+    mine = left.at[x, y, :, top, wide]
     x5 = [sender.start(mine, mine, dev) for _, dev in py]
     settle(y4)
-    mine = left.at[x, y, :, :, cy]
+    mine = left.at[x, y, :, low16, wide]
     y5 = [sender.start(mine, mine, dev) for _, dev in px]
-    settle(z4)
-    mine = left.at[x, :, z, :, cz]
-    z5 = [sender.start(mine, mine, dev) for _, dev in px]
-
+
+    settle(z5)
+    mine = left.at[:, :, z, :, narrow]
+    z6 = {d: sender.start(mine, mine, on_z(d)[1]) for d in (1, -1, 2, -2)}
     settle(x5)
-    mine = left.at[x, :, :, :, cx]
+    mine = left.at[x, :, :, top, wide]
     x6 = [sender.start(mine, mine, dev) for _, dev in px]
     settle(y5)
-    mine = left.at[:, y, :, :, cy]
+    mine = left.at[:, y, :, low16, wide]
     y6 = [sender.start(mine, mine, dev) for _, dev in py]
-    settle(z5)
-    mine = left.at[:, :, z, :, cz]
-    z6 = [sender.start(mine, mine, dev) for _, dev in pz]
-    settle(x6 + y6 + z6)
+    z7 = []
+    for k, d in enumerate((1, -1)):
+        z6[2 * d].wait()
+        source, _ = on_z(-2 * d)
+        piece = left.at[:, :, source, :, narrow]
+        z7.append(sender.start(piece, piece, on_z(d)[1]))
+        piece = left.at[halves[k], :, source, :, narrow]
+        z7.append(sender.start(piece, piece, on_z(2 * d)[1]))
+    z6[1].wait()
+    z6[-1].wait()
+    settle(z7 + x6 + y6)
 
     gsend[...] = jnp.zeros_like(gsend)
     tpart[...] = jnp.zeros_like(tpart)
 
-    def products(i, _):
-        xi, half = lax.div(i, 2), lax.rem(i, 2)
-        block = left[xi, pl.ds(half * 2, 2)].reshape(512, R)
-        rows = pl.ds(pl.multiple_of(i * 512, 512), 512)
-        gsend[...] += lax.dot_general(
-            block, block, (((0,), (0,)), ((), ())), preferred_element_type=F32
-        )
-        tpart[...] += lax.dot_general(
-            low[rows, :], block, (((0,), (0,)), ((), ())), preferred_element_type=F32
-        ).reshape(tpart.shape)
+    def products(xi, _):
+        block = left[xi].reshape(1024, R)
+        over_rows = (((0,), (0,)), ((), ()))
+        gsend[...] += lax.dot_general(block, block, over_rows, preferred_element_type=F32)
+        value = lax.dot_general(low[xi], block, over_rows, preferred_element_type=F32)
+        tpart[...] += value.reshape(tpart.shape)
         return 0
 
-    lax.fori_loop(0, 8, products, 0)
+    lax.fori_loop(0, NX, products, 0)
     g1 = sender.start(gsend, grecv, sibling)
-    around = peers("pair")
     t1 = [sender.start(tpart.at[p], trecv.at[k], dev) for k, (p, dev) in enumerate(around)]
     me = x * 2 + c
     mine = right.at[me]
@@ -346,24 +376,23 @@
     own[...] = jnp.broadcast_to(jnp.sum(mean * mean, axis=0, keepdims=True), own.shape)
     y7 = [sender.start(own, ry.at[k], dev) for k, (_, dev) in enumerate(py)]
 
-    def ortho(i, _):
-        xi, yi = lax.div(i, NY), lax.rem(i, NY)
-        block = left[xi, yi].reshape(NZ * ROWS, R)
+    def ortho(xi, _):
+        block = left[xi].reshape(1024, R)
         high = inverse[...].astype(BF16)
         rest = grecv[...].astype(BF16)
         value = nt(block, high, None) + nt(block, rest, None)
-        left[xi, yi] = value.astype(BF16).reshape(NZ, ROWS, R)
+        left[xi] = value.astype(BF16).reshape(NY, NZ, ROWS, R)
         return 0
 
-    lax.fori_loop(0, NX * NY // 2, ortho, 0)
+    lax.fori_loop(0, NX // 2, ortho, 0)
     settle(y7)
     value = own[...]
     for k in range(NY - 1):
         value = value + ry[k]
     mid[...] = value
-    z7 = [sender.start(mid, rz.at[k], dev) for k, (_, dev) in enumerate(pz)]
-    lax.fori_loop(NX * NY // 2, NX * NY, ortho, 0)
-    settle(z7)
+    z8 = [sender.start(mid, rz.at[k], dev) for k, (_, dev) in enumerate(pz)]
+    lax.fori_loop(NX // 2, NX, ortho, 0)
+    settle(z8)
     value = mid[...]
     for k in range(NZ - 1):
         value = value + rz[k]
@@ -380,24 +409,29 @@
 def front(momentum, gradient, basis):
     vmem = pl.BlockSpec(memory_space=pltpu.VMEM)
     scratch = [
-        pltpu.VMEM((LOCAL_ROWS, COLS), BF16),
+        pltpu.VMEM((NX, 1024, COLS), F32),
+        pltpu.VMEM((NX, 1024, COLS), BF16),
+        pltpu.VMEM((NX, 1024, COLS), BF16),
         pltpu.VMEM((2, COLS, 256), BF16),
         pltpu.VMEM((NX, NY, NZ, ROWS, R), BF16),
-        pltpu.VMEM((3, NY, NZ, ROWS, 256), BF16),
-        pltpu.VMEM((3, NX, NZ, ROWS, 128), BF16),
-        pltpu.VMEM((7, NX, NY, ROWS, 128), BF16),
-        pltpu.VMEM((NY, NZ, ROWS, 256), BF16),
-        pltpu.VMEM((NX, NZ, ROWS, 128), BF16),
-        pltpu.VMEM((NX, NY, ROWS, 128), BF16),
-        pltpu.VMEM((3, NZ, ROWS, 256), BF16),
-        pltpu.VMEM((3, NZ, ROWS, 128), BF16),
-        pltpu.VMEM((3, NY, ROWS, 128), BF16),
-        pltpu.VMEM((NZ, ROWS, 256), BF16),
-        pltpu.VMEM((NZ, ROWS, 128), BF16),
-        pltpu.VMEM((NY, ROWS, 128), BF16),
-        pltpu.VMEM((7, ROWS, 256), BF16),
-        pltpu.VMEM((7, ROWS, 128), BF16),
-        pltpu.VMEM((3, ROWS, 128), BF16),
+        pltpu.VMEM((3, NY, NZ, 16, WIDE), BF16),
+        pltpu.VMEM((3, NX, NZ, 16, WIDE), BF16),
+        pltpu.VMEM((2, NX, NY, ROWS, R - WIDE), BF16),
+        pltpu.VMEM((4, NX, NY, ROWS, R - WIDE), BF16),
+        pltpu.VMEM((2, 2, NY, ROWS, R - WIDE), BF16),
+        pltpu.VMEM((2, NX, NY, ROWS, R - WIDE), BF16),
+        pltpu.VMEM((NY, NZ, 16, WIDE), BF16),
+        pltpu.VMEM((NX, NZ, 16, WIDE), BF16),
+        pltpu.VMEM((NX, NY, ROWS, R - WIDE), BF16),
+        pltpu.VMEM((3, NZ, 16, WIDE), BF16),
+        pltpu.VMEM((3, NZ, 16, WIDE), BF16),
+        pltpu.VMEM((3, NY, ROWS, R - WIDE), BF16),
+        pltpu.VMEM((NZ, 16, WIDE), BF16),
+        pltpu.VMEM((NZ, 16, WIDE), BF16),
+        pltpu.VMEM((NY, ROWS, R - WIDE), BF16),
+        pltpu.VMEM((7, 16, WIDE), BF16),
+        pltpu.VMEM((7, 16, WIDE), BF16),
+        pltpu.VMEM((3, ROWS, R - WIDE), BF16),
         pltpu.VMEM((R, R), F32),
         pltpu.VMEM((R, R), F32),
         pltpu.VMEM((8, 32, R), F32),
@@ -409,6 +443,7 @@
         pltpu.VMEM((3, 8, R), F32),
         pltpu.VMEM((8, R), F32),
         pltpu.VMEM((7, 8, R), F32),
+        pltpu.SemaphoreType.DMA((8,)),
         pltpu.SemaphoreType.DMA((112,)),
         pltpu.SemaphoreType.DMA((112,)),
     ]
@@ -420,11 +455,11 @@
             jax.ShapeDtypeStruct((COLS, R), BF16),
             jax.ShapeDtypeStruct((COLS, 256), F32),
         ),
-        in_specs=[vmem] * 3,
+        in_specs=[pl.BlockSpec(memory_space=pl.ANY)] * 2 + [vmem],
         out_specs=(vmem,) * 4,
         scratch_shapes=scratch,
         compiler_params=pltpu.CompilerParams(
-            collective_id=0, has_side_effects=True, vmem_limit_bytes=56 * MIB
+            collective_id=0, has_side_effects=True, vmem_limit_bytes=60 * MIB
         ),
         name="front",
     )(momentum, gradient, basis)
@@ -454,7 +489,7 @@
         ),
         in_specs=[rows, whole((COLS, R)), whole((COLS, R)), cube, cube],
         out_specs=(cube, pl.BlockSpec((tile, COLS), lambda i: (i, 0))),
-        compiler_params=pltpu.CompilerParams(vmem_limit_bytes=40 * MIB),
+        compiler_params=pltpu.CompilerParams(vmem_limit_bytes=60 * MIB),
         name="finish",
     )(left, right, following, momentum, gradient)
 

time: 149 us -> 132 us (0.89); the launches traced: 147 us -> 132 us
  Pallas kernels: 141 us -> 131 us
  local copies, waits for them, and re-layouts: 4.79 us -> 0.71 us
    pallas_call x1, Pallas kernels: 135 us -> 120 us  [front(): pl.pallas_call(front_kernel, out_shape=(jax.ShapeDtypeStruct((NX, NY, NZ,...]
    pallas_call x1, Pallas kernels: 5.84 us -> 10.6 us  [finish(): pl.pallas_call(finish_kernel, grid=(LOCAL_ROWS // tile,), out_shape=(jax....]
    unnamed x13 -> x3, local copies, waits for them, and re-layouts: 4.79 us -> 0.71 us
where the time goes in v3:
time: 132 us
  Pallas kernels  131 us (99%)
    pallas_call x1, Pallas kernels, front(): pl.pallas_call(front_kernel, out_shape=(jax.ShapeDtypeStruct((NX, NY, NZ,...  120 us
    pallas_call x1, Pallas kernels, finish(): pl.pallas_call(finish_kernel, grid=(LOCAL_ROWS // tile,), out_shape=(jax....  10.6 us

profile of v3, /device:TPU:6, one launch (start us, length us, event | category | flops | bytes accessed | tf_op | source)
XLA Modules:
  0.0 131.9 jit_solution(1391811144313689059)
XLA Ops:
  0.6 119.9 %front.1 = (bf16[4,4,8,32,512]{4,3,2,1,0:T(8,128)(2,1)}, bf16[256,512]{1,0:T(8,128)(2,1)}, bf16[256,512]{1,0:T(8,128)(2,1)}, f32[256,256]{1,0:T(8,128)}) custom-call(f32[1,4096,256]{2,1,0:T(8,128)} %mom.1, bf16[1,4096,256]{2,1,0:T(8,128)(2,1)} %grad.1, f32[256,256]{1,0:T(8,128)} %basis.1), custom_call_target="tpu_custom_call" | custom-call | tf_op jit(solution)/shard_map/front/pallas_call | solution.py:450
  120.6 0.0 copy-start
  120.6 10.6 %finish.1 = (f32[1,4096,256]{2,1,0:T(8,128)}, bf16[4096,256]{1,0:T(8,128)(2,1)}) custom-call(bf16[4096,512]{1,0:T(8,128)(2,1)} %bitcast.1, bf16[256,512]{1,0:T(8,128)(2,1)} %get-tuple-element.10.right, bf16[256,512]{1,0:T(8,128)(2,1)} %get-tuple-element.11.following, f32[1,4096,256]{2,1,0:T(8,128)} %mom.1, bf16[1,4096,256]{2,1,0:T(8,128)(2,1)} %grad.1), custom_call_target="tpu_custom_call" | custom-call | tf_op jit(solution)/shard_map/finish/pallas_call | solution.py:483
  131.2 0.0 copy-done
  131.2 0.7 copy.7
Async XLA Ops:
  120.6 10.6 %copy-start = (f32[256,256]{1,0:T(8,128)S(1)}, f32[256,256]{1,0:T(8,128)}, u32[]{:S(2)}) copy-start(f32[256,256]{1,0:T(8,128)} %get-tuple-element.19) | copy-start | bytes 786436

commit v4 on v3

--- a/solution.py
+++ b/solution.py
@@ -88,52 +88,46 @@
     n=16
     sub=lax.broadcasted_iota(jnp.int32,(8,128),0)
     lane=lax.broadcasted_iota(jnp.int32,(8,128),1)
-    G=[load(g) for g in range(n)]
-    Y=[(lane==sub+8*g).astype(F32) for g in range(n)]
+    M=[load(g) for g in range(n)]
     out=[]
     for p in range(n):
         at=8*p
-        C=[jnp.broadcast_to(G[p][:,at+k:at+k+1],(8,128)) for k in range(8)]
+        inside=(lane>=at)&(lane<at+8)
+        ident=(lane==sub+at).astype(F32)
+        C=[jnp.broadcast_to(M[p][:,at+k:at+k+1],(8,128)) for k in range(8)]
         c={(i,k): splat_rows(C[k],i) for k in range(8) for i in range(k,8)}
+        g0=jnp.where(inside,ident,M[p])
+        grow=[splat_rows(g0,i) for i in range(8)]
         r=[None]*8; l={}
+        us=[]
+        done=jnp.zeros((8,128),F32)
         for j in range(8):
-            piv=c[j,j]
-            rr=lax.rsqrt(piv)
-            rr=rr*(1.5-0.5*piv*rr*rr)
+            rr=lax.rsqrt(c[j,j])
             r[j]=rr
             for i in range(j+1,8): l[i,j]=c[i,j]*rr
             for k in range(j+1,8):
                 for i in range(k,8):
                     c[i,k]=c[i,k]-l[i,j]*l[k,j]
-        us,ys=[],[]
-        g0,y0=G[p],Y[p]
-        done_y=jnp.zeros((8,128),F32)
-        Lc=[]
-        for j in range(8):
-            col=C[j]
-            for i in range(j): col=col-Lc[i]*l[j,i]
-            col=col*r[j]
-            Lc.append(col)
-            u=splat_rows(g0,j)*r[j]
-            yv=splat_rows(y0,j)*r[j]
-            us.append(u); ys.append(yv)
-            m=jnp.where(sub>j,col,0.0)
-            g0=g0-m*u
-            y0=y0-m*yv
-            done_y=jnp.where(sub==j,yv,done_y)
-        out.append(done_y)
-        for g in range(p+1,n):
-            Cg=[jnp.broadcast_to(G[g][:,at+k:at+k+1],(8,128)) for k in range(8)]
+            t=grow[j]
+            for k in range(j): t=t-l[j,k]*us[k]
+            u=t*rr
+            us.append(u)
+            done=jnp.where(sub==j,u,done)
+        out.append(done)
+        def by_columns(g):
+            Cg=[jnp.broadcast_to(M[g][:,at+k:at+k+1],(8,128)) for k in range(8)]
             L=[]
-            gg,yy=G[g],Y[g]
+            gg=jnp.where(inside,0.0,M[g])
             for j in range(8):
                 col=Cg[j]
                 for i in range(j): col=col-L[i]*l[j,i]
                 col=col*r[j]; L.append(col)
                 gg=gg-col*us[j]
-                yy=yy-col*ys[j]
-            G[g],Y[g]=gg,yy
-    return out
+            M[g]=gg
+        for g in range(p+1,n):
+            by_columns(g)
+    return [jnp.where(lane<=sub+8*g,out[g],0.0) for g in range(n)]
+
 
 def nt(a, b, precision=HIGH):
     return lax.dot_general(
@@ -172,10 +166,10 @@
 
 
 def front_kernel(
-    momentum, gradient, basis, left, right_low, next_low, new_basis,
-    mom, grad, low, base, part, rx1, ry1, za, zb, zh, zs, sx1, sy1, sz1, rx2, ry2, rz2, sx2, sy2, sz2,
+    momentum, gradient, basis, ortho_out, right_low, next_low, new_basis,
+    left, mom, grad, low, base, part, rx1, ry1, za, zb, zh, zs, sx1, sy1, sz1, rx2, ry2, rz2, sx2, sy2, sz2,
     rx3, ry3, rz3, gsend, grecv, tpart, trecv, right, inverse, following, own, ry, mid, rz,
-    load, send, recv,
+    load, store, send, recv,
 ):
     x, c, y, z = place()
     sender = Sender(send, recv)
@@ -196,21 +190,26 @@
         two.start()
         loads.append((one, two))
     base[c] = basis[...].astype(BF16)
-    pl.semaphore_wait(barrier, len(greeted))
-    basis_copy = sender.start(base.at[c], base.at[c], sibling)
-
-    top, low16 = pl.ds(0, 16), pl.ds(16, 16)
-    wide, narrow = pl.ds(0, WIDE), pl.ds(WIDE, R - WIDE)
-    x1 = []
+
+    def product(p, h):
+        value = jnp.dot(low[p], base[h], preferred_element_type=F32).astype(BF16)
+        columns = pl.ds(pl.multiple_of(h * 256, 256), 256)
+        part[p, :, :, :, columns] = value.reshape(NY, NZ, ROWS, 256)
+
     for k, p in enumerate(order):
         for copy in loads[k]:
             copy.wait()
         low[p] = (mom[p] + grad[p].astype(F32)).astype(BF16)
-        if k == 0:
-            basis_copy.wait()
-        for h in range(2):
-            value = jnp.dot(low[p], base[h], preferred_element_type=F32).astype(BF16)
-            part[p, :, :, :, h * 256 : (h + 1) * 256] = value.reshape(NY, NZ, ROWS, 256)
+        product(p, c)
+    pl.semaphore_wait(barrier, len(greeted))
+    basis_copy = sender.start(base.at[c], base.at[c], sibling)
+
+    top, low16 = pl.ds(0, 16), pl.ds(16, 16)
+    wide, narrow = pl.ds(0, WIDE), pl.ds(WIDE, R - WIDE)
+    x1 = []
+    basis_copy.wait()
+    for k, p in enumerate(order):
+        product(p, 1 - c)
         if k < NX - 1:
             dev = px[k][1]
             x1.append(sender.start(part.at[p, :, :, top, wide], rx1.at[k], dev))
@@ -338,22 +337,33 @@
     gsend[...] = jnp.zeros_like(gsend)
     tpart[...] = jnp.zeros_like(tpart)
 
-    def products(xi, _):
+    over_rows = (((0,), (0,)), ((), ()))
+
+    def gram_of(xi, _):
         block = left[xi].reshape(1024, R)
-        over_rows = (((0,), (0,)), ((), ()))
         gsend[...] += lax.dot_general(block, block, over_rows, preferred_element_type=F32)
+        return 0
+
+    def right_of(xi, _):
+        block = left[xi].reshape(1024, R)
         value = lax.dot_general(low[xi], block, over_rows, preferred_element_type=F32)
         tpart[...] += value.reshape(tpart.shape)
         return 0
 
-    lax.fori_loop(0, NX, products, 0)
-    g1 = sender.start(gsend, grecv, sibling)
+    lax.fori_loop(0, NX, gram_of, 0)
+    below, first = pl.ds(256, 256), pl.ds(0, 256)
+    g1 = [
+        sender.start(gsend.at[below, :], grecv.at[below, :], sibling),
+        sender.start(gsend.at[first, first], grecv.at[first, first], sibling),
+    ]
+    lax.fori_loop(0, NX, right_of, 0)
     t1 = [sender.start(tpart.at[p], trecv.at[k], dev) for k, (p, dev) in enumerate(around)]
     me = x * 2 + c
     mine = right.at[me]
     t2 = [sender.make(mine, mine, dev) for _, dev in around]
-    g1.wait()
-    gsend[...] = gsend[...] + grecv[...]
+    settle(g1)
+    gsend[256:512, :] = gsend[256:512, :] + grecv[256:512, :]
+    gsend[0:256, 0:256] = gsend[0:256, 0:256] + grecv[0:256, 0:256]
 
     def between(kb):
         @pl.when(kb == 2)
@@ -382,6 +392,7 @@
         rest = grecv[...].astype(BF16)
         value = nt(block, high, None) + nt(block, rest, None)
         left[xi] = value.astype(BF16).reshape(NY, NZ, ROWS, R)
+        pltpu.make_async_copy(left.at[xi], ortho_out.at[xi], store.at[xi]).start()
         return 0
 
     lax.fori_loop(0, NX // 2, ortho, 0)
@@ -405,10 +416,14 @@
         def _():
             new_basis[...] = following[:, core * 256 : (core + 1) * 256]
 
+    for xi in range(NX):
+        pltpu.make_async_copy(left.at[xi], ortho_out.at[xi], store.at[xi]).wait()
+
 
 def front(momentum, gradient, basis):
     vmem = pl.BlockSpec(memory_space=pltpu.VMEM)
     scratch = [
+        pltpu.VMEM((NX, NY, NZ, ROWS, R), BF16),
         pltpu.VMEM((NX, 1024, COLS), F32),
         pltpu.VMEM((NX, 1024, COLS), BF16),
         pltpu.VMEM((NX, 1024, COLS), BF16),
@@ -444,6 +459,7 @@
         pltpu.VMEM((8, R), F32),
         pltpu.VMEM((7, 8, R), F32),
         pltpu.SemaphoreType.DMA((8,)),
+        pltpu.SemaphoreType.DMA((NX,)),
         pltpu.SemaphoreType.DMA((112,)),
         pltpu.SemaphoreType.DMA((112,)),
     ]
@@ -456,7 +472,7 @@
             jax.ShapeDtypeStruct((COLS, 256), F32),
         ),
         in_specs=[pl.BlockSpec(memory_space=pl.ANY)] * 2 + [vmem],
-        out_specs=(vmem,) * 4,
+        out_specs=(pl.BlockSpec(memory_space=pl.ANY),) + (vmem,) * 3,
         scratch_shapes=scratch,
         compiler_params=pltpu.CompilerParams(
             collective_id=0, has_side_effects=True, vmem_limit_bytes=60 * MIB
@@ -476,7 +492,7 @@
 
 
 def finish(left, right, following, momentum, gradient):
-    tile = 512
+    tile = 2048
     whole = lambda shape: pl.BlockSpec(shape, lambda i: (0,) * len(shape))
     rows = pl.BlockSpec((tile, R), lambda i: (i, 0))
     cube = pl.BlockSpec((1, tile, COLS), lambda i: (0, i, 0))

time: 132 us -> 123 us (0.932)
  Pallas kernels: 131 us -> 121 us
    pallas_call x1, Pallas kernels: 120 us -> 114 us  [front(): pl.pallas_call(front_kernel, out_shape=(jax.ShapeDtypeStruct((NX, NY, NZ,...]
    pallas_call x1, Pallas kernels: 10.6 us -> 7.52 us  [finish(): pl.pallas_call(finish_kernel, grid=(LOCAL_ROWS // tile,), out_shape=(jax....]
where the time goes in v4:
time: 123 us
  Pallas kernels  121 us (98%)
    pallas_call x1, Pallas kernels, front(): pl.pallas_call(front_kernel, out_shape=(jax.ShapeDtypeStruct((NX, NY, NZ,...  114 us
    pallas_call x1, Pallas kernels, finish(): pl.pallas_call(finish_kernel, grid=(LOCAL_ROWS // tile,), out_shape=(jax....  7.52 us

profile of v4, /device:TPU:6, one launch (start us, length us, event | category | flops | bytes accessed | tf_op | source)
XLA Modules:
  0.0 122.6 jit_solution(3785329019356136851)
XLA Ops:
  0.6 113.7 %front.1 = (bf16[4,4,8,32,512]{4,3,2,1,0:T(8,128)(2,1)}, bf16[256,512]{1,0:T(8,128)(2,1)}, bf16[256,512]{1,0:T(8,128)(2,1)}, f32[256,256]{1,0:T(8,128)}) custom-call(f32[1,4096,256]{2,1,0:T(8,128)} %mom.1, bf16[1,4096,256]{2,1,0:T(8,128)(2,1)} %grad.1, f32[256,256]{1,0:T(8,128)} %basis.1), custom_call_target="tpu_custom_call" | custom-call | tf_op jit(solution)/shard_map/front/pallas_call | solution.py:466
  114.3 0.0 copy-start
  114.3 7.5 %finish.1 = (f32[1,4096,256]{2,1,0:T(8,128)}, bf16[4096,256]{1,0:T(8,128)(2,1)}) custom-call(bf16[4096,512]{1,0:T(8,128)(2,1)} %bitcast.1, bf16[256,512]{1,0:T(8,128)(2,1)} %get-tuple-element.10.right, bf16[256,512]{1,0:T(8,128)(2,1)} %get-tuple-element.11.following, f32[1,4096,256]{2,1,0:T(8,128)} %mom.1, bf16[1,4096,256]{2,1,0:T(8,128)(2,1)} %grad.1), custom_call_target="tpu_custom_call" | custom-call | tf_op jit(solution)/shard_map/finish/pallas_call | solution.py:499
  121.9 0.0 copy-done
  121.9 0.7 copy.7
Async XLA Ops:
  114.3 7.5 %copy-start = (f32[256,256]{1,0:T(8,128)S(1)}, f32[256,256]{1,0:T(8,128)}, u32[]{:S(2)}) copy-start(f32[256,256]{1,0:T(8,128)} %get-tuple-element.19) | copy-start | bytes 786436

commit v5 on v4

--- a/solution.py
+++ b/solution.py
@@ -168,7 +168,7 @@
 def front_kernel(
     momentum, gradient, basis, ortho_out, right_low, next_low, new_basis,
     left, mom, grad, low, base, part, rx1, ry1, za, zb, zh, zs, sx1, sy1, sz1, rx2, ry2, rz2, sx2, sy2, sz2,
-    rx3, ry3, rz3, gsend, grecv, tpart, trecv, right, inverse, following, own, ry, mid, rz,
+    rx3, ry3, rz3, gsend, grecv, tpart, trecv, right, inverse, halved, following, own, ry, mid, rz,
     load, store, send, recv,
 ):
     x, c, y, z = place()
@@ -339,9 +339,18 @@
 
     over_rows = (((0,), (0,)), ((), ()))
 
-    def gram_of(xi, _):
+    def gram_below(xi, _):
         block = left[xi].reshape(1024, R)
-        gsend[...] += lax.dot_general(block, block, over_rows, preferred_element_type=F32)
+        gsend[256:512, :] += lax.dot_general(
+            block[:, 256:512], block, over_rows, preferred_element_type=F32
+        )
+        return 0
+
+    def gram_first(xi, _):
+        block = left[xi, :, :, :, 0:256].reshape(1024, 256)
+        gsend[0:256, 0:256] += lax.dot_general(
+            block, block, over_rows, preferred_element_type=F32
+        )
         return 0
 
     def right_of(xi, _):
@@ -350,12 +359,11 @@
         tpart[...] += value.reshape(tpart.shape)
         return 0
 
-    lax.fori_loop(0, NX, gram_of, 0)
     below, first = pl.ds(256, 256), pl.ds(0, 256)
-    g1 = [
-        sender.start(gsend.at[below, :], grecv.at[below, :], sibling),
-        sender.start(gsend.at[first, first], grecv.at[first, first], sibling),
-    ]
+    lax.fori_loop(0, NX, gram_below, 0)
+    g1 = [sender.start(gsend.at[below, :], grecv.at[below, :], sibling)]
+    lax.fori_loop(0, NX, gram_first, 0)
+    g1.append(sender.start(gsend.at[first, first], grecv.at[first, first], sibling))
     lax.fori_loop(0, NX, right_of, 0)
     t1 = [sender.start(tpart.at[p], trecv.at[k], dev) for k, (p, dev) in enumerate(around)]
     me = x * 2 + c
@@ -377,20 +385,22 @@
                 copy.start()
 
     inverse_factor(gsend, inverse, between)
-    grecv[...] = inverse[...] - inverse[...].astype(BF16).astype(F32)
+    halved[0] = inverse[...].astype(BF16)
+    halved[1] = (inverse[...] - inverse[...].astype(BF16).astype(F32)).astype(BF16)
     settle(t2)
 
     mean = nt(right[...].reshape(COLS, R), inverse[...])
     right_low[...] = mean.astype(BF16)
     following[...] = mean
-    own[...] = jnp.broadcast_to(jnp.sum(mean * mean, axis=0, keepdims=True), own.shape)
+    squares = jnp.sum(mean * mean, axis=0, keepdims=True)
+    own[...] = jnp.zeros_like(own)
+    for q in range(R // 128):
+        own[q : q + 1, :] = squares[:, q * 128 : (q + 1) * 128]
     y7 = [sender.start(own, ry.at[k], dev) for k, (_, dev) in enumerate(py)]
 
     def ortho(xi, _):
         block = left[xi].reshape(1024, R)
-        high = inverse[...].astype(BF16)
-        rest = grecv[...].astype(BF16)
-        value = nt(block, high, None) + nt(block, rest, None)
+        value = nt(block, halved[0], None) + nt(block, halved[1], None)
         left[xi] = value.astype(BF16).reshape(NY, NZ, ROWS, R)
         pltpu.make_async_copy(left.at[xi], ortho_out.at[xi], store.at[xi]).start()
         return 0
@@ -407,7 +417,8 @@
     value = mid[...]
     for k in range(NZ - 1):
         value = value + rz[k]
-    scale = 1.0 / jnp.sqrt(value[0:1] / D + 1e-05)
+    squares = jnp.concatenate([value[q : q + 1] for q in range(R // 128)], axis=1)
+    scale = 1.0 / jnp.sqrt(squares / D + 1e-05)
     following[...] = following[...] * scale
     next_low[...] = following[...].astype(BF16)
     for core in range(2):
@@ -453,11 +464,12 @@
         pltpu.VMEM((7, 32, R), F32),
         pltpu.VMEM((8, 32, R), F32),
         pltpu.VMEM((R, R), F32),
+        pltpu.VMEM((2, R, R), BF16),
         pltpu.VMEM((COLS, R), F32),
-        pltpu.VMEM((8, R), F32),
-        pltpu.VMEM((3, 8, R), F32),
-        pltpu.VMEM((8, R), F32),
-        pltpu.VMEM((7, 8, R), F32),
+        pltpu.VMEM((8, 128), F32),
+        pltpu.VMEM((3, 8, 128), F32),
+        pltpu.VMEM((8, 128), F32),
+        pltpu.VMEM((7, 8, 128), F32),
         pltpu.SemaphoreType.DMA((8,)),
         pltpu.SemaphoreType.DMA((NX,)),
         pltpu.SemaphoreType.DMA((112,)),
@@ -481,7 +493,8 @@
     )(momentum, gradient, basis)
 
 
-def finish_kernel(left, right, following, mom, grad, new_mom, update):
+def finish_kernel(left, right, following, basis, mom, grad, new_mom, new_basis, update):
+    new_basis[...] = basis[...]
     ortho = left[...]
     across = (((1,), (1,)), ((), ()))
     lowrank = lax.dot_general(ortho, right[...], across, preferred_element_type=F32)
@@ -491,7 +504,7 @@
     update[...] = (product * factor).astype(BF16)
 
 
-def finish(left, right, following, momentum, gradient):
+def finish(left, right, following, basis, momentum, gradient):
     tile = 2048
     whole = lambda shape: pl.BlockSpec(shape, lambda i: (0,) * len(shape))
     rows = pl.BlockSpec((tile, R), lambda i: (i, 0))
@@ -501,21 +514,19 @@
         grid=(LOCAL_ROWS // tile,),
         out_shape=(
             jax.ShapeDtypeStruct((1, LOCAL_ROWS, COLS), F32),
+            jax.ShapeDtypeStruct((COLS, 256), F32),
             jax.ShapeDtypeStruct((LOCAL_ROWS, COLS), BF16),
         ),
-        in_specs=[rows, whole((COLS, R)), whole((COLS, R)), cube, cube],
-        out_specs=(cube, pl.BlockSpec((tile, COLS), lambda i: (i, 0))),
+        in_specs=[rows, whole((COLS, R)), whole((COLS, R)), whole((COLS, 256)), cube, cube],
+        out_specs=(cube, whole((COLS, 256)), pl.BlockSpec((tile, COLS), lambda i: (i, 0))),
         compiler_params=pltpu.CompilerParams(vmem_limit_bytes=60 * MIB),
         name="finish",
-    )(left, right, following, momentum, gradient)
+    )(left, right, following, basis, momentum, gradient)
 
 
 def shards(momentum, gradient, basis):
     ortho, right, following, new_basis = front(momentum, gradient, basis)
-    new_momentum, update = finish(
-        ortho.reshape(LOCAL_ROWS, R), right, following, momentum, gradient
-    )
-    return (new_momentum, new_basis, update)
+    return finish(ortho.reshape(LOCAL_ROWS, R), right, following, new_basis, momentum, gradient)
 
 
 def solution(mesh):

time: 123 us -> 121 us (0.984)
    pallas_call x1, Pallas kernels: 114 us -> 112 us  [front(): pl.pallas_call(front_kernel, out_shape=(jax.ShapeDtypeStruct((NX, NY, NZ,...]
where the time goes in v5:
time: 121 us; the launch traced here: 120 us
  Pallas kernels  120 us (99%)
    pallas_call x1, Pallas kernels, front(): pl.pallas_call(front_kernel, out_shape=(jax.ShapeDtypeStruct((NX, NY, NZ,...  112 us
    pallas_call x1, Pallas kernels, finish(): pl.pallas_call(finish_kernel, grid=(LOCAL_ROWS // tile,), out_shape=(jax....  7.61 us

profile of v5, /device:TPU:6, one launch (start us, length us, event | category | flops | bytes accessed | tf_op | source)
XLA Modules:
  0.0 120.5 jit_solution(831308378222778085)
XLA Ops:
  0.6 112.2 %front.1 = (bf16[4,4,8,32,512]{4,3,2,1,0:T(8,128)(2,1)}, bf16[256,512]{1,0:T(8,128)(2,1)}, bf16[256,512]{1,0:T(8,128)(2,1)}, f32[256,256]{1,0:T(8,128)}) custom-call(f32[1,4096,256]{2,1,0:T(8,128)} %mom.1, bf16[1,4096,256]{2,1,0:T(8,128)(2,1)} %grad.1, f32[256,256]{1,0:T(8,128)} %basis.1), custom_call_target="tpu_custom_call" | custom-call | tf_op jit(solution)/shard_map/front/pallas_call | solution.py:478
  112.9 7.6 %finish.1 = (f32[1,4096,256]{2,1,0:T(8,128)}, f32[256,256]{1,0:T(8,128)}, bf16[4096,256]{1,0:T(8,128)(2,1)}) custom-call(bf16[4096,512]{1,0:T(8,128)(2,1)} %bitcast.1, bf16[256,512]{1,0:T(8,128)(2,1)} %get-tuple-element.8.right, bf16[256,512]{1,0:T(8,128)(2,1)} %get-tuple-element.9.following, f32[256,256]{1,0:T(8,128)} %get-tuple-element.10.basis, ...), custom_call_target="tpu_custom_call" | custom-call | tf_op jit(solution)/shard_map/finish/pallas_call | solution.py:512

commit v6 on v5

--- a/solution.py
+++ b/solution.py
@@ -487,7 +487,7 @@
         out_specs=(pl.BlockSpec(memory_space=pl.ANY),) + (vmem,) * 3,
         scratch_shapes=scratch,
         compiler_params=pltpu.CompilerParams(
-            collective_id=0, has_side_effects=True, vmem_limit_bytes=60 * MIB
+            collective_id=0, has_side_effects=True, vmem_limit_bytes=40 * MIB
         ),
         name="front",
     )(momentum, gradient, basis)
@@ -519,7 +519,7 @@
         ),
         in_specs=[rows, whole((COLS, R)), whole((COLS, R)), whole((COLS, 256)), cube, cube],
         out_specs=(cube, whole((COLS, 256)), pl.BlockSpec((tile, COLS), lambda i: (i, 0))),
-        compiler_params=pltpu.CompilerParams(vmem_limit_bytes=60 * MIB),
+        compiler_params=pltpu.CompilerParams(vmem_limit_bytes=24 * MIB),
         name="finish",
     )(left, right, following, basis, momentum, gradient)
 

time: 121 us -> 120 us (level)
  Pallas kernels: 120 us -> 115 us
  local copies, waits for them, and re-layouts: 0 us -> 4.72 us
    unnamed x0 -> x6, local copies, waits for them, and re-layouts: none -> 4.72 us
    pallas_call x1, Pallas kernels: 7.61 us -> 4.33 us  [finish(): pl.pallas_call(finish_kernel, grid=(LOCAL_ROWS // tile,), out_shape=(jax....]
    pallas_call x1, Pallas kernels: 112 us -> 110 us  [front(): pl.pallas_call(front_kernel, out_shape=(jax.ShapeDtypeStruct((NX, NY, NZ,...]
where the time goes in v6:
time: 120 us
  Pallas kernels  115 us (96%)
  local copies, waits for them, and re-layouts  4.72 us (4%)
    pallas_call x1, Pallas kernels, front(): pl.pallas_call(front_kernel, out_shape=(jax.ShapeDtypeStruct((NX, NY, NZ,...  110 us
    unnamed x6, local copies, waits for them, and re-layouts  4.72 us
    pallas_call x1, Pallas kernels, finish(): pl.pallas_call(finish_kernel, grid=(LOCAL_ROWS // tile,), out_shape=(jax....  4.33 us

profile of v6, /device:TPU:6, one launch (start us, length us, event | category | flops | bytes accessed | tf_op | source)
XLA Modules:
  0.0 120.1 jit_solution(16618253873231716381)
XLA Ops:
  0.6 0.0 copy-start
  0.6 2.2 %copy-done = f32[1,4096,256]{2,1,0:T(8,128)S(1)} copy-done((f32[1,4096,256]{2,1,0:T(8,128)S(1)}, f32[1,4096,256]{2,1,0:T(8,128)}, u32[]{:S(2)}) %copy-start) | copy-done | bytes 4194328
  2.8 0.0 copy-start.1
  2.8 1.6 %copy-done.1 = bf16[1,4096,256]{2,1,0:T(8,128)(2,1)S(1)} copy-done((bf16[1,4096,256]{2,1,0:T(8,128)(2,1)S(1)}, bf16[1,4096,256]{2,1,0:T(8,128)(2,1)}, u32[]{:S(2)}) %copy-start.1) | copy-done | bytes 2097176
  4.4 0.0 copy-start.2
  4.4 0.9 copy-done.2
  5.4 110.4 %front.1 = (bf16[4,4,8,32,512]{4,3,2,1,0:T(8,128)(2,1)S(1)}, bf16[256,512]{1,0:T(8,128)(2,1)S(1)}, bf16[256,512]{1,0:T(8,128)(2,1)S(1)}, f32[256,256]{1,0:T(8,128)S(1)}) custom-call(f32[1,4096,256]{2,1,0:T(8,128)S(1)} %copy-done, bf16[1,4096,256]{2,1,0:T(8,128)(2,1)S(1)} %copy-done.1, f32[256,256]{1,0:T(8,128)S(1)} %copy-done.2), custom_call_target="tpu_custom_call" | custom-call | tf_op jit(solution)/shard_map/front/pallas_call | solution.py:478
  115.8 4.3 %finish.1 = (f32[1,4096,256]{2,1,0:T(8,128)}, f32[256,256]{1,0:T(8,128)}, bf16[4096,256]{1,0:T(8,128)(2,1)}) custom-call(bf16[4096,512]{1,0:T(8,128)(2,1)S(1)} %bitcast.1, bf16[256,512]{1,0:T(8,128)(2,1)S(1)} %get-tuple-element.8.right, bf16[256,512]{1,0:T(8,128)(2,1)S(1)} %get-tuple-element.9.following, f32[256,256]{1,0:T(8,128)S(1)} %get-tuple-element.10.basis, ...), custom_call_target="tpu_custom_call" | custom-call | tf_op jit(solution)/shard_map/finish/pallas_call | solution.py:512
Async XLA Ops:
  0.6 2.2 %copy-start = (f32[1,4096,256]{2,1,0:T(8,128)S(1)}, f32[1,4096,256]{2,1,0:T(8,128)}, u32[]{:S(2)}) copy-start(f32[1,4096,256]{2,1,0:T(8,128)} %mom.1) | copy-start | bytes 12582916
  2.8 1.6 %copy-start.1 = (bf16[1,4096,256]{2,1,0:T(8,128)(2,1)S(1)}, bf16[1,4096,256]{2,1,0:T(8,128)(2,1)}, u32[]{:S(2)}) copy-start(bf16[1,4096,256]{2,1,0:T(8,128)(2,1)} %grad.1) | copy-start | bytes 6291460
  4.4 0.9 copy-start.2
